TPU v7x, 32 devices: a whole 2x2x4 slice. The times are simulated.
32 devices in a mesh: height: 4 (over x, core), width: 4 (over z), head: 2 (over y).
Axes of the slice: x: 2, y: 2, z: 4, core: 2. Of those that a mesh axis runs over, the one named last changes fastest.
Arguments:
- tokens: bfloat16 [4, 8, 144, 1536], P('height', 'width'), may hold values from -6 to 6
- grad_out: bfloat16 [4, 8, 144, 1536], P('height', 'width'), may hold values from -6 to 6
- qkv_weight: bfloat16 [1536, 3, 768], P(('height', 'width'), None, 'head'), may hold values from -0.15625 to 0.15625
- out_weight: bfloat16 [1536, 768], P(('height', 'width'), 'head'), may hold values from -0.5 to 0.5
- q_gain: float32 [768], P('head'), may hold values from 0.5 to 2
- k_gain: float32 [768], P('head'), may hold values from 0.5 to 2
- key_valid: int32 [4, 8, 144], P('height', 'width'), may hold values from 0 to 1, as said below
Outputs:
- mixed: bfloat16 [4, 8, 144, 1536], P('height', 'width', None, 'head')
- grad_in: bfloat16 [4, 8, 144, 1536], P('height', 'width', None, 'head')
Inputs may be any that keep to these rules, and one draw needn't show every extreme that they name: key_valid is 0 only in the last row of tiles and in the last column of tiles. In a tile of the last row, each frame and column within the tile has its own count of valid rows, 1 to 5, and the rows from that count on are 0. In a tile of the last column, each frame and row within the tile has its own count of valid columns, 1 to 8, and the columns from that count on are 0. The first token of every tile is valid.
All inputs are finite; a program needn't handle non-finite values.
Results may differ from a plain program's by a relative error of at most 0.015.
Values may be sent and summed in bfloat16 or wider, within the bound.
A program may use at most 128 MiB of HBM per device.

v0:
```python
import jax
import jax.numpy as jnp
from jax import lax
from jax.sharding import PartitionSpec as P

HEAD_DIM = 128


epsilon = 1e-06


def padded(x, sides, width):
    for axis, dim in sides:
        count, length = (lax.axis_size(axis), x.shape[dim])
        up = [(i, (i + 1) % count) for i in range(count - 1)]
        down = [(j, i) for i, j in up]
        last = lax.slice_in_dim(x, length - width, length, axis=dim)
        first = lax.slice_in_dim(x, 0, width, axis=dim)
        before = lax.ppermute(last, axis, up)
        after = lax.ppermute(first, axis, down)
        x = jnp.concatenate([before, x, after], axis=dim)
    return x


def norm_scale(raw_values, gain_vec):
    inverse = lax.rsqrt(jnp.mean(raw_values * raw_values, axis=-1, keepdims=True) + epsilon)
    return (raw_values * inverse * gain_vec, inverse)


def norm_backward(raw_values, inverse, gain_vec, upstream):
    weighted = gain_vec * upstream
    inner_mean = jnp.mean(weighted * raw_values, axis=-1, keepdims=True)
    return inverse * weighted - raw_values * inverse**3 * inner_mean


def windows(extended, tile_rows, tile_cols):
    return jnp.stack(
        [
            extended[row_step : row_step + tile_rows, col_step : col_step + tile_cols]
            for row_step in range(3)
            for col_step in range(3)
        ],
        axis=2,
    )


def fold_windows(windowed, tile_rows, tile_cols):
    total = jnp.zeros((tile_rows + 2, tile_cols + 2) + windowed.shape[3:], jnp.float32)
    for position in range(9):
        row_step, col_step = divmod(position, 3)
        total = total.at[row_step : row_step + tile_rows, col_step : col_step + tile_cols].add(
            windowed[:, :, position]
        )
    return total


def fold_along(values, along, length):
    middle = lax.slice_in_dim(values, 2, length + 2, axis=along)
    first_rim = lax.slice_in_dim(values, 0, 1, axis=along)
    last_rim = lax.slice_in_dim(values, length + 3, length + 4, axis=along)
    before = [(0, 0)] * values.ndim
    before[along] = (0, length - 1)
    behind = [(0, 0)] * values.ndim
    behind[along] = (length - 1, 0)
    return middle + jnp.pad(first_rim, before) + jnp.pad(last_rim, behind)


def attend(queries, win_keys, win_values, win_valid, upstream):
    factor = HEAD_DIM ** (-0.5)
    scores = (
        jnp.einsum("bqhe,bkhe->bhqk", queries, win_keys, preferred_element_type=jnp.float32)
        * factor
    )
    weights = jnp.exp(scores) * win_valid[:, None, None, :]
    attn_probs = weights / jnp.sum(weights, axis=-1, keepdims=True)
    attn_weights = attn_probs.astype(jnp.bfloat16)
    attended = jnp.einsum(
        "bhqk,bkhe->bqhe", attn_weights, win_values, preferred_element_type=jnp.float32
    ).astype(jnp.bfloat16)
    grad_probs = jnp.einsum(
        "bqhe,bkhe->bhqk", upstream, win_values, preferred_element_type=jnp.float32
    )
    grad_scores = attn_probs * (
        grad_probs - jnp.sum(attn_probs * grad_probs, axis=-1, keepdims=True)
    )
    grad_scores = grad_scores.astype(jnp.bfloat16)
    grad_values = jnp.einsum(
        "bhqk,bqhe->bkhe", attn_weights, upstream, preferred_element_type=jnp.float32
    )
    grad_keys = (
        jnp.einsum("bhqk,bqhe->bkhe", grad_scores, queries, preferred_element_type=jnp.float32)
        * factor
    )
    grad_queries = (
        jnp.einsum("bhqk,bkhe->bqhe", grad_scores, win_keys, preferred_element_type=jnp.float32)
        * factor
    )
    return (attended, grad_queries, grad_keys, grad_values)


def on_device(tokens, grad_out, qkv_weight, out_weight, q_gain, k_gain, key_valid):
    tile_rows, tile_cols, tile_tokens, model_width = tokens.shape
    head_count = q_gain.shape[0] // HEAD_DIM
    inner_width = head_count * HEAD_DIM
    token_count = tile_rows * tile_cols * tile_tokens
    tile_count = tile_rows * tile_cols
    whole_qkv, whole_out = (
        lax.all_gather(qkv_weight, ("height", "width"), axis=0, tiled=True),
        lax.all_gather(out_weight, ("height", "width"), axis=0, tiled=True),
    )
    projected = jnp.dot(
        tokens.reshape(token_count, model_width),
        whole_qkv.reshape(model_width, 3 * inner_width),
        preferred_element_type=jnp.float32,
    ).reshape(token_count, 3, head_count, HEAD_DIM)
    q_gains = q_gain.reshape(head_count, HEAD_DIM)
    k_gains = k_gain.reshape(head_count, HEAD_DIM)
    q_normed, q_inverse = norm_scale(projected[:, 0], q_gains)
    k_normed, k_inverse = norm_scale(projected[:, 1], k_gains)
    shape_tiles = (tile_rows, tile_cols, tile_tokens, head_count, HEAD_DIM)
    queries = q_normed.astype(jnp.bfloat16).reshape(tile_count, tile_tokens, head_count, HEAD_DIM)
    keys_tiled = k_normed.astype(jnp.bfloat16).reshape(shape_tiles)
    values_tiled = projected[:, 2].astype(jnp.bfloat16).reshape(shape_tiles)
    keys_ext, values_ext, valid_ext = (
        padded(keys_tiled, (("height", 0), ("width", 1)), 1),
        padded(values_tiled, (("height", 0), ("width", 1)), 1),
        padded(key_valid.astype(jnp.bfloat16), (("height", 0), ("width", 1)), 1),
    )
    win_keys = windows(keys_ext, tile_rows, tile_cols).reshape(
        tile_count, 9 * tile_tokens, head_count, HEAD_DIM
    )
    win_values = windows(values_ext, tile_rows, tile_cols).reshape(
        tile_count, 9 * tile_tokens, head_count, HEAD_DIM
    )
    win_valid = (
        windows(valid_ext, tile_rows, tile_cols)
        .reshape(tile_count, 9 * tile_tokens)
        .astype(jnp.float32)
    )
    grad_attended = jnp.dot(
        grad_out.reshape(token_count, model_width), whole_out, preferred_element_type=jnp.float32
    )
    grad_attended = grad_attended.astype(jnp.bfloat16).reshape(
        tile_count, tile_tokens, head_count, HEAD_DIM
    )
    attended, grad_queries, grad_keys_win, grad_values_win = attend(
        queries, win_keys, win_values, win_valid, grad_attended
    )
    win_shape = (tile_rows, tile_cols, 9, tile_tokens, head_count, HEAD_DIM)
    keys_back = fold_windows(grad_keys_win.reshape(win_shape), tile_rows, tile_cols)
    values_back = fold_windows(grad_values_win.reshape(win_shape), tile_rows, tile_cols)
    keys_recv, values_recv = (
        padded(keys_back.astype(jnp.bfloat16), (("height", 0), ("width", 1)), 1).astype(
            keys_back.dtype
        ),
        padded(values_back.astype(jnp.bfloat16), (("height", 0), ("width", 1)), 1).astype(
            values_back.dtype
        ),
    )
    grad_keys = fold_along(fold_along(keys_recv, 0, tile_rows), 1, tile_cols)
    grad_values = fold_along(fold_along(values_recv, 0, tile_rows), 1, tile_cols)
    grad_q_raw = norm_backward(
        projected[:, 0], q_inverse, q_gains, grad_queries.reshape(token_count, head_count, HEAD_DIM)
    )
    grad_k_raw = norm_backward(
        projected[:, 1], k_inverse, k_gains, grad_keys.reshape(token_count, head_count, HEAD_DIM)
    )
    grad_qkv = jnp.stack(
        [grad_q_raw, grad_k_raw, grad_values.reshape(token_count, head_count, HEAD_DIM)], axis=1
    )
    grad_qkv = grad_qkv.reshape(token_count, 3, inner_width).astype(jnp.bfloat16)
    attended_rows = attended.reshape(token_count, inner_width)
    mixed_part = jnp.dot(attended_rows, whole_out.T, preferred_element_type=jnp.float32)
    mixed = lax.psum_scatter(
        mixed_part.astype(jnp.bfloat16), "head", scatter_dimension=1, tiled=True
    )
    grad_part = jnp.dot(
        grad_qkv.reshape(token_count, 3 * inner_width),
        whole_qkv.reshape(model_width, 3 * inner_width).T,
        preferred_element_type=jnp.float32,
    )
    grad_in = lax.psum_scatter(
        grad_part.astype(jnp.bfloat16), "head", scatter_dimension=1, tiled=True
    )
    out_shape = (tile_rows, tile_cols, tile_tokens, -1)
    return (mixed.reshape(out_shape), grad_in.reshape(out_shape))


def solution(mesh):
    placed = (
        P("height", "width", None, None),
        P("height", "width", None, None),
        P(("height", "width"), None, "head"),
        P(("height", "width"), "head"),
        P("head"),
        P("head"),
        P("height", "width", None),
    )
    return jax.shard_map(
        on_device,
        mesh=mesh,
        in_specs=placed,
        out_specs=(P("height", "width", None, "head"), P("height", "width", None, "head")),
        check_vma=False,
    )
```

profile of v0, /device:TPU:9, one launch (start us, length us, event | category | flops | bytes accessed | tf_op | source)
XLA Modules:
  0.0 232.6 jit_solution(3244571344516373420)
XLA Ops:
  8.6 2.6 %collective-permute-start.9 = (bf16[1,2,144]{2,1,0:T(2,128)(2,1)S(1)}, bf16[1,2,144]{2,1,0:T(2,128)(2,1)S(1)}, u32[]{:S(2)}, u32[]{:S(2)}) collective-permute-start(bf16[1,2,144]{2,1,0:T(2,128)(2,1)S(1)} %convert_element_type.105), channel_id=1, source_target_pairs={{8,0},{16,8},{24,16},{9,1},{17,9},{25,17},{10,2},{18,10},{26,18},{... | collective-permute-start | bytes 1736 | tf_op jit(solution)/shard_map/ppermute | solution.py:20
  11.2 3.0 %collective-permute-start.8 = (bf16[1,2,144]{2,1,0:T(2,128)(2,1)S(1)}, bf16[1,2,144]{2,1,0:T(2,128)(2,1)S(1)}, u32[]{:S(2)}, u32[]{:S(2)}) collective-permute-start(bf16[1,2,144]{2,1,0:T(2,128)(2,1)S(1)} %convert_element_type.105), channel_id=1, source_target_pairs={{0,8},{8,16},{16,24},{1,9},{9,17},{17,25},{2,10},{10,18},{18,26},{... | collective-permute-start | bytes 1736 | tf_op jit(solution)/shard_map/ppermute | solution.py:19
  16.4 3.2 %collective-permute-start.10 = (bf16[3,1,144]{2,1,0:T(2,128)(2,1)S(1)}, bf16[3,1,144]{2,1,0:T(2,128)(2,1)S(1)}, u32[]{:S(2)}, u32[]{:S(2)}) collective-permute-start(bf16[3,1,144]{2,1,0:T(2,128)(2,1)S(1)} %get-tuple-element.243), channel_id=1, source_target_pairs={{0,2},{2,4},{4,6},{1,3},{3,5},{5,7},{8,10},{10,12},{12,14},{9,11},... | collective-permute-start | bytes 2600 | tf_op jit(solution)/shard_map/ppermute | solution.py:19
  22.3 2.6 %collective-permute-done.11 = bf16[3,1,144]{2,1,0:T(2,128)(2,1)S(1)} collective-permute-done((bf16[3,1,144]{2,1,0:T(2,128)(2,1)S(1)}, bf16[3,1,144]{2,1,0:T(2,128)(2,1)S(1)}, u32[]{:S(2)}, u32[]{:S(2)}) %collective-permute-start.11) | collective-permute-done | bytes 896 | tf_op jit(solution)/shard_map/ppermute | solution.py:20
  25.9 33.9 %all-gather.3.cloned.1.call-done = bf16[1536,3,384]{2,0,1:T(8,128)(2,1)} async-done(((bf16[96,3,384]{2,0,1:T(8,128)(2,1)}), bf16[1536,3,384]{2,0,1:T(8,128)(2,1)}) %all-gather.3.cloned.1.call-update) | async-done | bytes 3538960 | tf_op jit(solution)/shard_map/all_gather | solution.py:108
  59.7 6.1 %copy.69 = bf16[1536,3,384]{0,2,1:T(8,128)(2,1)} copy(bf16[1536,3,384]{2,0,1:T(8,128)(2,1)} %all-gather.3.cloned.1.call-done) | data formatting | bytes 7077888 | tf_op jit(solution)/shard_map/all_gather | solution.py:108
  65.8 3.3 %fusion.105 = f32[288,3,3,128]{3,0,2,1:T(8,128)S(1)} fusion(bf16[288,1536,1,1]{1,0,3,2:T(8,128)(2,1)S(1)} %bitcast.318, bf16[3,3,128,1536]{3,2,1,0:T(8,128)(2,1)} %bitcast.356), kind=kOutput, calls=%fused_computation.213 | convolution fusion | flops 1019215872 | bytes 5750784 | tf_op jit(solution)/shard_map/dot_general | solution.py:111
  71.4 2.2 collective-permute-start.5
  73.5 3.4 %collective-permute-start.4 = (bf16[1,2,144,3,128]{4,2,1,3,0:T(8,128)(2,1)S(1)}, bf16[1,2,144,3,128]{4,2,1,3,0:T(8,128)(2,1)S(1)}, u32[]{:S(2)}, u32[]{:S(2)}) collective-permute-start(bf16[1,2,144,3,128]{4,2,1,3,0:T(8,128)(2,1)S(1)} %multiply_convert_fusion.2), channel_id=1, source_target_pairs={{0,8},{8,16},{16,24},{1,9},{9,17},{17,25},{2,10},{10,18},{18,26},{... | collective-permute-start | bytes 663560 | tf_op jit(solution)/shard_map/ppermute | solution.py:19
  76.9 21.0 %all-gather.5.cloned.1.call-done = bf16[1536,384]{1,0:T(8,128)(2,1)} async-done(((bf16[96,384]{1,0:T(8,128)(2,1)}), bf16[1536,384]{1,0:T(8,128)(2,1)}) %all-gather.5.cloned.1.call-update) | async-done | bytes 1179664 | tf_op jit(solution)/shard_map/all_gather | solution.py:109
  97.9 2.2 convolution_convert_fusion.1
  100.2 2.2 collective-permute-start.1
  102.4 3.4 %collective-permute-start = (bf16[1,2,144,3,128]{4,2,1,3,0:T(8,128)(2,1)S(1)}, bf16[1,2,144,3,128]{4,2,1,3,0:T(8,128)(2,1)S(1)}, u32[]{:S(2)}, u32[]{:S(2)}) collective-permute-start(bf16[1,2,144,3,128]{4,2,1,3,0:T(8,128)(2,1)S(1)} %bitcast.324), channel_id=1, source_target_pairs={{0,8},{8,16},{16,24},{1,9},{9,17},{17,25},{2,10},{10,18},{18,26},{... | collective-permute-start | bytes 663560 | tf_op jit(solution)/shard_map/ppermute | solution.py:19
  106.0 2.3 %collective-permute-start.6 = (bf16[3,1,144,3,128]{4,2,1,3,0:T(8,128)(2,1)S(1)}, bf16[3,1,144,3,128]{4,2,1,3,0:T(8,128)(2,1)S(1)}, u32[]{:S(2)}, u32[]{:S(2)}) collective-permute-start(bf16[3,1,144,3,128]{4,2,1,3,0:T(8,128)(2,1)S(1)} %get-tuple-element.235), channel_id=1, source_target_pairs={{0,2},{2,4},{4,6},{1,3},{3,5},{5,7},{8,10},{10,12},{12,14},{9,11},... | collective-permute-start | bytes 995336 | tf_op jit(solution)/shard_map/ppermute | solution.py:19
  108.8 3.1 %collective-permute-start.3 = (bf16[3,1,144,3,128]{4,2,1,3,0:T(8,128)(2,1)S(1)}, bf16[3,1,144,3,128]{4,2,1,3,0:T(8,128)(2,1)S(1)}, u32[]{:S(2)}, u32[]{:S(2)}) collective-permute-start(bf16[3,1,144,3,128]{4,2,1,3,0:T(8,128)(2,1)S(1)} %get-tuple-element.236), channel_id=1, source_target_pairs={{2,0},{4,2},{6,4},{3,1},{5,3},{7,5},{10,8},{12,10},{14,12},{11,9},... | collective-permute-start | bytes 995336 | tf_op jit(solution)/shard_map/ppermute | solution.py:20
  111.9 2.4 %collective-permute-start.2 = (bf16[3,1,144,3,128]{4,2,1,3,0:T(8,128)(2,1)S(1)}, bf16[3,1,144,3,128]{4,2,1,3,0:T(8,128)(2,1)S(1)}, u32[]{:S(2)}, u32[]{:S(2)}) collective-permute-start(bf16[3,1,144,3,128]{4,2,1,3,0:T(8,128)(2,1)S(1)} %get-tuple-element.237), channel_id=1, source_target_pairs={{0,2},{2,4},{4,6},{1,3},{3,5},{5,7},{8,10},{10,12},{12,14},{9,11},... | collective-permute-start | bytes 995336 | tf_op jit(solution)/shard_map/ppermute | solution.py:19
  114.2 3.1 %collective-permute-start.7 = (bf16[3,1,144,3,128]{4,2,1,3,0:T(8,128)(2,1)S(1)}, bf16[3,1,144,3,128]{4,2,1,3,0:T(8,128)(2,1)S(1)}, u32[]{:S(2)}, u32[]{:S(2)}) collective-permute-start(bf16[3,1,144,3,128]{4,2,1,3,0:T(8,128)(2,1)S(1)} %get-tuple-element.234), channel_id=1, source_target_pairs={{2,0},{4,2},{6,4},{3,1},{5,3},{7,5},{10,8},{12,10},{14,12},{11,9},... | collective-permute-start | bytes 995336 | tf_op jit(solution)/shard_map/ppermute | solution.py:20
  117.7 9.2 %collective-permute-done.7 = bf16[3,1,144,3,128]{4,2,1,3,0:T(8,128)(2,1)S(1)} collective-permute-done((bf16[3,1,144,3,128]{4,2,1,3,0:T(8,128)(2,1)S(1)}, bf16[3,1,144,3,128]{4,2,1,3,0:T(8,128)(2,1)S(1)}, u32[]{:S(2)}, u32[]{:S(2)}) %collective-permute-start.7) | collective-permute-done | bytes 331808 | tf_op jit(solution)/shard_map/ppermute | solution.py:20
  129.3 3.1 %fusion.88 = f32[2,3,144,1296]{3,2,1,0:T(8,128)} fusion(bf16[2,1296,3,128]{3,1,2,0:T(8,128)(2,1)S(1)} %bitcast.321, bf16[2,144,3,128]{3,2,1,0:T(4,128)(2,1)S(1)} %reshape.1031), kind=kOutput, calls=%fused_computation.171 | convolution fusion | flops 286654464 | bytes 6690816 | tf_op jit(solution)/shard_map/bqhe,bkhe->bhqk/dot_general | solution.py:80
  132.4 7.1 %multiply_reduce_fusion = (f32[2,3,144]{2,1,0:T(4,128)S(1)}, f32[2,3,144,1296]{3,2,1,0:T(8,128)}) fusion(f32[2,3,144,1296]{3,2,1,0:T(8,128)} %fusion.88, bf16[2,1296,3,128]{3,1,2,0:T(8,128)(2,1)} %bitcast.351, f32[2,1296]{1,0:T(2,128)S(1)} %reshape.1059, f32[2,144,3,128]{3,1,0,2:T(8,128)S(1)} %bitcast.357, f32[3,128]{1,0:T(4,128)S(1)} %bitcast.361, ...), kind=kOutput, calls=%fused_computation.1 | convolution fusion | flops 292586240 | bytes 11409792 | tf_op jit(solution)/shard_map/div | solution.py:75
  139.5 3.4 %fusion.13 = bf16[2,144,3,128]{3,1,2,0:T(8,128)(2,1)S(1)} fusion(bf16[2,1296,3,128]{3,1,2,0:T(8,128)(2,1)S(1)} %bitcast.322, f32[2,3,144,1296]{3,2,1,0:T(8,128)} %get-tuple-element.251), kind=kOutput, calls=%fused_computation.21 | convolution fusion | flops 287884800 | bytes 6690816 | tf_op jit(solution)/shard_map/bhqk,bkhe->bqhe/dot_general | solution.py:77
  151.6 2.3 %collective-permute-start.12 = (bf16[1,4,144,3,128]{4,2,3,1,0:T(8,128)(2,1)S(1)}, bf16[1,4,144,3,128]{4,2,3,1,0:T(8,128)(2,1)S(1)}, u32[]{:S(2)}, u32[]{:S(2)}) collective-permute-start(bf16[1,4,144,3,128]{4,2,3,1,0:T(8,128)(2,1)S(1)} %get-tuple-element.228), channel_id=1, source_target_pairs={{0,8},{8,16},{16,24},{1,9},{9,17},{17,25},{2,10},{10,18},{18,26},{... | collective-permute-start | bytes 1327112 | tf_op jit(solution)/shard_map/ppermute | solution.py:19
  160.6 3.7 %collective-permute-start.16 = (bf16[1,4,144,3,128]{4,2,3,1,0:T(8,128)(2,1)S(1)}, bf16[1,4,144,3,128]{4,2,3,1,0:T(8,128)(2,1)S(1)}, u32[]{:S(2)}, u32[]{:S(2)}) collective-permute-start(bf16[1,4,144,3,128]{4,2,3,1,0:T(8,128)(2,1)S(1)} %get-tuple-element.230), channel_id=1, source_target_pairs={{0,8},{8,16},{16,24},{1,9},{9,17},{17,25},{2,10},{10,18},{18,26},{... | collective-permute-start | bytes 1327112 | tf_op jit(solution)/shard_map/ppermute | solution.py:19
  169.2 3.4 %collective-permute-start.14 = (bf16[5,1,144,3,128]{4,2,3,1,0:T(8,128)(2,1)}, bf16[5,1,144,3,128]{4,2,3,1,0:T(8,128)(2,1)}, u32[]{:S(2)}, u32[]{:S(2)}) collective-permute-start(bf16[5,1,144,3,128]{4,2,3,1,0:T(8,128)(2,1)} %get-tuple-element.222), channel_id=1, source_target_pairs={{0,2},{2,4},{4,6},{1,3},{3,5},{5,7},{8,10},{10,12},{12,14},{9,11},... | collective-permute-start | bytes 1658888 | tf_op jit(solution)/shard_map/ppermute | solution.py:19
  172.6 2.8 %collective-permute-start.15 = (bf16[5,1,144,3,128]{4,2,3,1,0:T(8,128)(2,1)}, bf16[5,1,144,3,128]{4,2,3,1,0:T(8,128)(2,1)}, u32[]{:S(2)}, u32[]{:S(2)}) collective-permute-start(bf16[5,1,144,3,128]{4,2,3,1,0:T(8,128)(2,1)} %get-tuple-element.223), channel_id=1, source_target_pairs={{2,0},{4,2},{6,4},{3,1},{5,3},{7,5},{10,8},{12,10},{14,12},{11,9},... | collective-permute-start | bytes 1658888 | tf_op jit(solution)/shard_map/ppermute | solution.py:20
  176.7 2.4 %collective-permute-start.18 = (bf16[5,1,144,3,128]{4,2,3,1,0:T(8,128)(2,1)}, bf16[5,1,144,3,128]{4,2,3,1,0:T(8,128)(2,1)}, u32[]{:S(2)}, u32[]{:S(2)}) collective-permute-start(bf16[5,1,144,3,128]{4,2,3,1,0:T(8,128)(2,1)} %get-tuple-element.224), channel_id=1, source_target_pairs={{0,2},{2,4},{4,6},{1,3},{3,5},{5,7},{8,10},{10,12},{12,14},{9,11},... | collective-permute-start | bytes 1658888 | tf_op jit(solution)/shard_map/ppermute | solution.py:19
  179.2 3.6 %collective-permute-start.19 = (bf16[5,1,144,3,128]{4,2,3,1,0:T(8,128)(2,1)}, bf16[5,1,144,3,128]{4,2,3,1,0:T(8,128)(2,1)}, u32[]{:S(2)}, u32[]{:S(2)}) collective-permute-start(bf16[5,1,144,3,128]{4,2,3,1,0:T(8,128)(2,1)} %get-tuple-element.225), channel_id=1, source_target_pairs={{2,0},{4,2},{6,4},{3,1},{5,3},{7,5},{10,8},{12,10},{14,12},{11,9},... | collective-permute-start | bytes 1658888 | tf_op jit(solution)/shard_map/ppermute | solution.py:20
  187.0 2.4 %collective-permute-done.15 = bf16[5,1,144,3,128]{4,2,3,1,0:T(8,128)(2,1)} collective-permute-done((bf16[5,1,144,3,128]{4,2,3,1,0:T(8,128)(2,1)}, bf16[5,1,144,3,128]{4,2,3,1,0:T(8,128)(2,1)}, u32[]{:S(2)}, u32[]{:S(2)}) %collective-permute-start.15) | collective-permute-done | bytes 552992 | tf_op jit(solution)/shard_map/ppermute | solution.py:20
  191.1 5.6 %collective-permute-done.18 = bf16[5,1,144,3,128]{4,2,3,1,0:T(8,128)(2,1)} collective-permute-done((bf16[5,1,144,3,128]{4,2,3,1,0:T(8,128)(2,1)}, bf16[5,1,144,3,128]{4,2,3,1,0:T(8,128)(2,1)}, u32[]{:S(2)}, u32[]{:S(2)}) %collective-permute-start.18) | collective-permute-done | bytes 552992 | tf_op jit(solution)/shard_map/ppermute | solution.py:19
  196.7 4.0 %collective-permute-done.19 = bf16[5,1,144,3,128]{4,2,3,1,0:T(8,128)(2,1)} collective-permute-done((bf16[5,1,144,3,128]{4,2,3,1,0:T(8,128)(2,1)}, bf16[5,1,144,3,128]{4,2,3,1,0:T(8,128)(2,1)}, u32[]{:S(2)}, u32[]{:S(2)}) %collective-permute-start.19) | collective-permute-done | bytes 552992 | tf_op jit(solution)/shard_map/ppermute | solution.py:20
  205.8 2.3 fusion
  208.1 17.9 %reduce-scatter.5.cloned.1.call-done = bf16[288,768]{1,0:T(8,128)(2,1)} async-done(((bf16[288,1536]{1,0:T(8,128)(2,1)}), bf16[288,768]{1,0:T(8,128)(2,1)}) %reduce-scatter.5.cloned.1.call-update) | async-done | bytes 442384 | tf_op jit(solution)/shard_map/reduce_scatter | solution.py:182
  (176 shorter events, 44.8 us)
Async XLA Ops:
  7.2 58.7 %copy-start = (bf16[1,2,144,1536]{3,2,1,0:T(8,128)(2,1)S(1)}, bf16[1,2,144,1536]{3,2,1,0:T(8,128)(2,1)}, u32[]{:S(2)}) copy-start(bf16[1,2,144,1536]{3,2,1,0:T(8,128)(2,1)} %param.43) | copy-start | bytes 2654212
  7.2 52.5 %all-gather.3.cloned.1.call-start = ((), (), s32[]{:S(2)}) async-start(), calls=%async_computation.2 | async-start | bytes 3760128 | tf_op jit(solution)/shard_map/all_gather | solution.py:108
  7.9 90.0 %all-gather.5.cloned.1.call-start = ((), (), s32[]{:S(2)}) async-start(), calls=%async_computation.3 | async-start | bytes 1253376 | tf_op jit(solution)/shard_map/all_gather | solution.py:109
  8.6 7.7 %collective-permute-start.9 = (bf16[1,2,144]{2,1,0:T(2,128)(2,1)S(1)}, bf16[1,2,144]{2,1,0:T(2,128)(2,1)S(1)}, u32[]{:S(2)}, u32[]{:S(2)}) collective-permute-start(bf16[1,2,144]{2,1,0:T(2,128)(2,1)S(1)} %convert_element_type.105), channel_id=1, source_target_pairs={{8,0},{16,8},{24,16},{9,1},{17,9},{25,17},{10,2},{18,10},{26,18},{... | collective-permute-start | bytes 1736 | tf_op jit(solution)/shard_map/ppermute | solution.py:20
  11.2 5.2 %collective-permute-start.8 = (bf16[1,2,144]{2,1,0:T(2,128)(2,1)S(1)}, bf16[1,2,144]{2,1,0:T(2,128)(2,1)S(1)}, u32[]{:S(2)}, u32[]{:S(2)}) collective-permute-start(bf16[1,2,144]{2,1,0:T(2,128)(2,1)S(1)} %convert_element_type.105), channel_id=1, source_target_pairs={{0,8},{8,16},{16,24},{1,9},{9,17},{17,25},{2,10},{10,18},{18,26},{... | collective-permute-start | bytes 1736 | tf_op jit(solution)/shard_map/ppermute | solution.py:19
  14.3 193.8 %reduce-scatter.3.cloned.1.call-start = ((), (), s32[]{:S(2)}) async-start(), calls=%async_computation.4 | async-start | bytes 1327104 | tf_op jit(solution)/shard_map/reduce_scatter | solution.py:174
  16.4 5.9 %collective-permute-start.10 = (bf16[3,1,144]{2,1,0:T(2,128)(2,1)S(1)}, bf16[3,1,144]{2,1,0:T(2,128)(2,1)S(1)}, u32[]{:S(2)}, u32[]{:S(2)}) collective-permute-start(bf16[3,1,144]{2,1,0:T(2,128)(2,1)S(1)} %get-tuple-element.243), channel_id=1, source_target_pairs={{0,2},{2,4},{4,6},{1,3},{3,5},{5,7},{8,10},{10,12},{12,14},{9,11},... | collective-permute-start | bytes 2600 | tf_op jit(solution)/shard_map/ppermute | solution.py:19
  20.2 4.7 %collective-permute-start.11 = (bf16[3,1,144]{2,1,0:T(2,128)(2,1)S(1)}, bf16[3,1,144]{2,1,0:T(2,128)(2,1)S(1)}, u32[]{:S(2)}, u32[]{:S(2)}) collective-permute-start(bf16[3,1,144]{2,1,0:T(2,128)(2,1)S(1)} %get-tuple-element.242), channel_id=1, source_target_pairs={{2,0},{4,2},{6,4},{3,1},{5,3},{7,5},{10,8},{12,10},{14,12},{11,9},... | collective-permute-start | bytes 2600 | tf_op jit(solution)/shard_map/ppermute | solution.py:20
  69.2 31.0 %copy-start.3 = (f32[288,3,3,128]{3,0,2,1:T(8,128)}, f32[288,3,3,128]{3,0,2,1:T(8,128)S(1)}, u32[]{:S(2)}) copy-start(f32[288,3,3,128]{3,0,2,1:T(8,128)S(1)} %fusion.105) | copy-start | bytes 3981316
  71.4 34.5 %collective-permute-start.5 = (bf16[1,2,144,3,128]{4,2,1,3,0:T(8,128)(2,1)S(1)}, bf16[1,2,144,3,128]{4,2,1,3,0:T(8,128)(2,1)S(1)}, u32[]{:S(2)}, u32[]{:S(2)}) collective-permute-start(bf16[1,2,144,3,128]{4,2,1,3,0:T(8,128)(2,1)S(1)} %multiply_convert_fusion.2), channel_id=1, source_target_pairs={{8,0},{16,8},{24,16},{9,1},{17,9},{25,17},{10,2},{18,10},{26,18},{... | collective-permute-start | bytes 663560 | tf_op jit(solution)/shard_map/ppermute | solution.py:20
  73.5 32.3 %collective-permute-start.4 = (bf16[1,2,144,3,128]{4,2,1,3,0:T(8,128)(2,1)S(1)}, bf16[1,2,144,3,128]{4,2,1,3,0:T(8,128)(2,1)S(1)}, u32[]{:S(2)}, u32[]{:S(2)}) collective-permute-start(bf16[1,2,144,3,128]{4,2,1,3,0:T(8,128)(2,1)S(1)} %multiply_convert_fusion.2), channel_id=1, source_target_pairs={{0,8},{8,16},{16,24},{1,9},{9,17},{17,25},{2,10},{10,18},{18,26},{... | collective-permute-start | bytes 663560 | tf_op jit(solution)/shard_map/ppermute | solution.py:19
  100.2 8.2 %collective-permute-start.1 = (bf16[1,2,144,3,128]{4,2,1,3,0:T(8,128)(2,1)S(1)}, bf16[1,2,144,3,128]{4,2,1,3,0:T(8,128)(2,1)S(1)}, u32[]{:S(2)}, u32[]{:S(2)}) collective-permute-start(bf16[1,2,144,3,128]{4,2,1,3,0:T(8,128)(2,1)S(1)} %bitcast.323), channel_id=1, source_target_pairs={{8,0},{16,8},{24,16},{9,1},{17,9},{25,17},{10,2},{18,10},{26,18},{... | collective-permute-start | bytes 663560 | tf_op jit(solution)/shard_map/ppermute | solution.py:20
  102.4 6.3 %collective-permute-start = (bf16[1,2,144,3,128]{4,2,1,3,0:T(8,128)(2,1)S(1)}, bf16[1,2,144,3,128]{4,2,1,3,0:T(8,128)(2,1)S(1)}, u32[]{:S(2)}, u32[]{:S(2)}) collective-permute-start(bf16[1,2,144,3,128]{4,2,1,3,0:T(8,128)(2,1)S(1)} %bitcast.324), channel_id=1, source_target_pairs={{0,8},{8,16},{16,24},{1,9},{9,17},{17,25},{2,10},{10,18},{18,26},{... | collective-permute-start | bytes 663560 | tf_op jit(solution)/shard_map/ppermute | solution.py:19
  106.0 11.6 %collective-permute-start.6 = (bf16[3,1,144,3,128]{4,2,1,3,0:T(8,128)(2,1)S(1)}, bf16[3,1,144,3,128]{4,2,1,3,0:T(8,128)(2,1)S(1)}, u32[]{:S(2)}, u32[]{:S(2)}) collective-permute-start(bf16[3,1,144,3,128]{4,2,1,3,0:T(8,128)(2,1)S(1)} %get-tuple-element.235), channel_id=1, source_target_pairs={{0,2},{2,4},{4,6},{1,3},{3,5},{5,7},{8,10},{10,12},{12,14},{9,11},... | collective-permute-start | bytes 995336 | tf_op jit(solution)/shard_map/ppermute | solution.py:19
  108.8 20.1 %collective-permute-start.3 = (bf16[3,1,144,3,128]{4,2,1,3,0:T(8,128)(2,1)S(1)}, bf16[3,1,144,3,128]{4,2,1,3,0:T(8,128)(2,1)S(1)}, u32[]{:S(2)}, u32[]{:S(2)}) collective-permute-start(bf16[3,1,144,3,128]{4,2,1,3,0:T(8,128)(2,1)S(1)} %get-tuple-element.236), channel_id=1, source_target_pairs={{2,0},{4,2},{6,4},{3,1},{5,3},{7,5},{10,8},{12,10},{14,12},{11,9},... | collective-permute-start | bytes 995336 | tf_op jit(solution)/shard_map/ppermute | solution.py:20
  111.9 17.0 %collective-permute-start.2 = (bf16[3,1,144,3,128]{4,2,1,3,0:T(8,128)(2,1)S(1)}, bf16[3,1,144,3,128]{4,2,1,3,0:T(8,128)(2,1)S(1)}, u32[]{:S(2)}, u32[]{:S(2)}) collective-permute-start(bf16[3,1,144,3,128]{4,2,1,3,0:T(8,128)(2,1)S(1)} %get-tuple-element.237), channel_id=1, source_target_pairs={{0,2},{2,4},{4,6},{1,3},{3,5},{5,7},{8,10},{10,12},{12,14},{9,11},... | collective-permute-start | bytes 995336 | tf_op jit(solution)/shard_map/ppermute | solution.py:19
  114.2 12.7 %collective-permute-start.7 = (bf16[3,1,144,3,128]{4,2,1,3,0:T(8,128)(2,1)S(1)}, bf16[3,1,144,3,128]{4,2,1,3,0:T(8,128)(2,1)S(1)}, u32[]{:S(2)}, u32[]{:S(2)}) collective-permute-start(bf16[3,1,144,3,128]{4,2,1,3,0:T(8,128)(2,1)S(1)} %get-tuple-element.234), channel_id=1, source_target_pairs={{2,0},{4,2},{6,4},{3,1},{5,3},{7,5},{10,8},{12,10},{14,12},{11,9},... | collective-permute-start | bytes 995336 | tf_op jit(solution)/shard_map/ppermute | solution.py:20
  151.6 16.4 %collective-permute-start.12 = (bf16[1,4,144,3,128]{4,2,3,1,0:T(8,128)(2,1)S(1)}, bf16[1,4,144,3,128]{4,2,3,1,0:T(8,128)(2,1)S(1)}, u32[]{:S(2)}, u32[]{:S(2)}) collective-permute-start(bf16[1,4,144,3,128]{4,2,3,1,0:T(8,128)(2,1)S(1)} %get-tuple-element.228), channel_id=1, source_target_pairs={{0,8},{8,16},{16,24},{1,9},{9,17},{17,25},{2,10},{10,18},{18,26},{... | collective-permute-start | bytes 1327112 | tf_op jit(solution)/shard_map/ppermute | solution.py:19
  154.0 14.1 %collective-permute-start.13 = (bf16[1,4,144,3,128]{4,2,3,1,0:T(8,128)(2,1)S(1)}, bf16[1,4,144,3,128]{4,2,3,1,0:T(8,128)(2,1)S(1)}, u32[]{:S(2)}, u32[]{:S(2)}) collective-permute-start(bf16[1,4,144,3,128]{4,2,3,1,0:T(8,128)(2,1)S(1)} %get-tuple-element.229), channel_id=1, source_target_pairs={{8,0},{16,8},{24,16},{9,1},{17,9},{25,17},{10,2},{18,10},{26,18},{... | collective-permute-start | bytes 1327112 | tf_op jit(solution)/shard_map/ppermute | solution.py:20
  160.6 14.9 %collective-permute-start.16 = (bf16[1,4,144,3,128]{4,2,3,1,0:T(8,128)(2,1)S(1)}, bf16[1,4,144,3,128]{4,2,3,1,0:T(8,128)(2,1)S(1)}, u32[]{:S(2)}, u32[]{:S(2)}) collective-permute-start(bf16[1,4,144,3,128]{4,2,3,1,0:T(8,128)(2,1)S(1)} %get-tuple-element.230), channel_id=1, source_target_pairs={{0,8},{8,16},{16,24},{1,9},{9,17},{17,25},{2,10},{10,18},{18,26},{... | collective-permute-start | bytes 1327112 | tf_op jit(solution)/shard_map/ppermute | solution.py:19
  164.3 11.2 %collective-permute-start.17 = (bf16[1,4,144,3,128]{4,2,3,1,0:T(8,128)(2,1)S(1)}, bf16[1,4,144,3,128]{4,2,3,1,0:T(8,128)(2,1)S(1)}, u32[]{:S(2)}, u32[]{:S(2)}) collective-permute-start(bf16[1,4,144,3,128]{4,2,3,1,0:T(8,128)(2,1)S(1)} %get-tuple-element.231), channel_id=1, source_target_pairs={{8,0},{16,8},{24,16},{9,1},{17,9},{25,17},{10,2},{18,10},{26,18},{... | collective-permute-start | bytes 1327112 | tf_op jit(solution)/shard_map/ppermute | solution.py:20
  169.2 13.6 %copy-start.14 = (bf16[1536,384]{1,0:T(8,128)(2,1)S(1)}, bf16[1536,384]{1,0:T(8,128)(2,1)}, u32[]{:S(2)}) copy-start(bf16[1536,384]{1,0:T(8,128)(2,1)} %all-gather.5.cloned.1.call-done) | copy-start | bytes 3538948
  169.2 17.8 %collective-permute-start.14 = (bf16[5,1,144,3,128]{4,2,3,1,0:T(8,128)(2,1)}, bf16[5,1,144,3,128]{4,2,3,1,0:T(8,128)(2,1)}, u32[]{:S(2)}, u32[]{:S(2)}) collective-permute-start(bf16[5,1,144,3,128]{4,2,3,1,0:T(8,128)(2,1)} %get-tuple-element.222), channel_id=1, source_target_pairs={{0,2},{2,4},{4,6},{1,3},{3,5},{5,7},{8,10},{10,12},{12,14},{9,11},... | collective-permute-start | bytes 1658888 | tf_op jit(solution)/shard_map/ppermute | solution.py:19
  172.6 16.7 %collective-permute-start.15 = (bf16[5,1,144,3,128]{4,2,3,1,0:T(8,128)(2,1)}, bf16[5,1,144,3,128]{4,2,3,1,0:T(8,128)(2,1)}, u32[]{:S(2)}, u32[]{:S(2)}) collective-permute-start(bf16[5,1,144,3,128]{4,2,3,1,0:T(8,128)(2,1)} %get-tuple-element.223), channel_id=1, source_target_pairs={{2,0},{4,2},{6,4},{3,1},{5,3},{7,5},{10,8},{12,10},{14,12},{11,9},... | collective-permute-start | bytes 1658888 | tf_op jit(solution)/shard_map/ppermute | solution.py:20
  175.5 8.9 %copy-start.9 = (bf16[1,4,144,3,128]{4,2,3,1,0:T(8,128)(2,1)}, bf16[1,4,144,3,128]{4,2,3,1,0:T(8,128)(2,1)S(1)}, u32[]{:S(2)}) copy-start(bf16[1,4,144,3,128]{4,2,3,1,0:T(8,128)(2,1)S(1)} %collective-permute-done.16) | copy-start | bytes 1327108
  176.7 19.9 %collective-permute-start.18 = (bf16[5,1,144,3,128]{4,2,3,1,0:T(8,128)(2,1)}, bf16[5,1,144,3,128]{4,2,3,1,0:T(8,128)(2,1)}, u32[]{:S(2)}, u32[]{:S(2)}) collective-permute-start(bf16[5,1,144,3,128]{4,2,3,1,0:T(8,128)(2,1)} %get-tuple-element.224), channel_id=1, source_target_pairs={{0,2},{2,4},{4,6},{1,3},{3,5},{5,7},{8,10},{10,12},{12,14},{9,11},... | collective-permute-start | bytes 1658888 | tf_op jit(solution)/shard_map/ppermute | solution.py:19
  179.2 21.5 %collective-permute-start.19 = (bf16[5,1,144,3,128]{4,2,3,1,0:T(8,128)(2,1)}, bf16[5,1,144,3,128]{4,2,3,1,0:T(8,128)(2,1)}, u32[]{:S(2)}, u32[]{:S(2)}) collective-permute-start(bf16[5,1,144,3,128]{4,2,3,1,0:T(8,128)(2,1)} %get-tuple-element.225), channel_id=1, source_target_pairs={{2,0},{4,2},{6,4},{3,1},{5,3},{7,5},{10,8},{12,10},{14,12},{11,9},... | collective-permute-start | bytes 1658888 | tf_op jit(solution)/shard_map/ppermute | solution.py:20
  185.5 40.6 %reduce-scatter.5.cloned.1.call-start = ((), (), s32[]{:S(2)}) async-start(), calls=%async_computation.5 | async-start | bytes 1327104 | tf_op jit(solution)/shard_map/reduce_scatter | solution.py:182
  187.0 13.7 %copy-start.10 = (bf16[1,4,144,3,128]{4,2,3,1,0:T(8,128)(2,1)S(1)}, bf16[1,4,144,3,128]{4,2,3,1,0:T(8,128)(2,1)}, u32[]{:S(2)}) copy-start(bf16[1,4,144,3,128]{4,2,3,1,0:T(8,128)(2,1)} %copy-done.9) | copy-start | bytes 1327108
  187.0 13.7 %copy-start.12 = (bf16[1,4,144,3,128]{4,2,3,1,0:T(8,128)(2,1)S(1)}, bf16[1,4,144,3,128]{4,2,3,1,0:T(8,128)(2,1)}, u32[]{:S(2)}) copy-start(bf16[1,4,144,3,128]{4,2,3,1,0:T(8,128)(2,1)} %copy-done.11) | copy-start | bytes 1327108
  191.1 11.2 %copy-start.21 = (pred[2]{0:T(512)(128)(4,1)S(1)}, pred[2]{0:T(512)(128)(4,1)}, u32[]{:S(2)}) copy-start(pred[2]{0:T(512)(128)(4,1)} %constant.473.clone.1) | copy-start | bytes 10
  205.8 20.3 %copy-start.1 = (bf16[1,2,144,1536]{3,2,1,0:T(8,128)(2,1)S(1)}, bf16[1,2,144,1536]{3,2,1,0:T(8,128)(2,1)}, u32[]{:S(2)}) copy-start(bf16[1,2,144,1536]{3,2,1,0:T(8,128)(2,1)} %param.43) | copy-start | bytes 2654212
  (16 other events, 46.1 us)
Sparse Core Ops, SparseCore 0:
  10.4 49.3 all-gather.2
  62.0 35.8 all-gather.4
  185.6 19.2 reduce-scatter.2
  208.2 17.8 reduce-scatter.4
where the time goes:
time: 235 us; the launch traced here: 233 us
  waiting for transfers between devices  97.9 us (42%)
  starting transfers between devices  55.5 us (24%)
  matrix products  27.7 us (12%)
  other arithmetic  22.3 us (9%)
  between operations  14.7 us (6%)
  local copies, waits for them, and re-layouts  14.5 us (6%)
    all_gather x1, waiting for transfers between devices, on_device(): lax.all_gather(qkv_weight, ('height', 'width'), axis=0, tiled=True)  33.9 us
    ppermute x10, starting transfers between devices, padded(): before = lax.ppermute(last, axis, up)  29.6 us
    ppermute x10, starting transfers between devices, padded(): after = lax.ppermute(first, axis, down)  25.8 us
    all_gather x1, waiting for transfers between devices, on_device(): lax.all_gather(out_weight, ('height', 'width'), axis=0, tiled=True)  21 us
    ppermute x10, waiting for transfers between devices, padded(): after = lax.ppermute(first, axis, down)  18.2 us
    reduce_scatter x1, waiting for transfers between devices, on_device(): lax.psum_scatter(grad_part.astype(jnp.bfloat16), 'head', scatter_dimensio...  17.9 us
    scatter-add x16, other arithmetic, fold_windows(): total.at[row_step:row_step + tile_rows, col_step:col_step + tile_cols]  7.91 us
    div x1, matrix products, attend(): attn_probs = weights / jnp.sum(weights, axis=-1, keepdims=True)  7.09 us
  transfers between devices with their start and end apart: 24, of which 10 were waited for; matrix products, arithmetic and copies ran while one was open for 17% of the time, Pallas kernels for 0%

commit v1 on v0

v1 whole, which is shorter than its diff:
```python
import functools

import jax
import jax.numpy as jnp
from jax import lax
from jax.experimental import pallas as pl
from jax.experimental.pallas import tpu as pltpu
from jax.sharding import PartitionSpec as P

HEAD_DIM = 128
EPS = 1e-06
FACTOR = HEAD_DIM**-0.5
LOG2E = 1.4426950408889634
ABSENT = 1e30
NT = (((1,), (1,)), ((), ()))
TN = (((0,), (0,)), ((), ()))
F32 = jnp.float32
BF16 = jnp.bfloat16


def mm(a, b, dims=(((1,), (0,)), ((), ()))):
    return lax.dot_general(a, b, dims, preferred_element_type=F32)


def body(cfg, *refs):
    nh, nw, heads, tt, gather = cfg
    tok, go, win, qg, kg, vcol, mixed, gin = refs[:8]
    rest = list(refs[8:])
    W = rest.pop(0) if gather else win
    (raw, ga, qb, kv, kc, gacc, att, gq, gs, gr, gs2, gr2, gqkv, ms, mr, ss, sr) = rest[:17]
    (s_h, r_h, s_g, r_g, s_y, r_y) = rest[17:23]
    width = heads * HEAD_DIM
    h, w, y = lax.axis_index("height"), lax.axis_index("width"), lax.axis_index("head")
    up, down, left, right = h > 0, h < nh - 1, w > 0, w < nw - 1
    peer = (h, w, 1 - y)
    dev = {"u": (h - 1, w, y), "d": (h + 1, w, y), "l": (h, w - 1, y), "r": (h, w + 1, y)}
    there = {"u": up, "d": down, "l": left, "r": right}
    xdev = (lax.rem(h + 2, nh), w, y)
    cdev = (h + 1 - 2 * lax.rem(h, 2), w, y)

    def copy(src, dst, ssem, rsem, to):
        return pltpu.make_async_remote_copy(
            src_ref=src, dst_ref=dst, send_sem=ssem, recv_sem=rsem,
            device_id=to, device_id_type=pl.DeviceIdType.MESH)

    barrier = pltpu.get_barrier_semaphore()

    def greet(to):
        pl.semaphore_signal(barrier, inc=1, device_id=to, device_id_type=pl.DeviceIdType.MESH)

    count = 1
    for side in "udlr":
        pl.when(there[side])(functools.partial(greet, dev[side]))
        count = count + there[side].astype(jnp.int32)
    greet(peer)
    if gather:
        greet(xdev)
        greet(cdev)
        count = count + 2
    pl.semaphore_wait(barrier, count)

    if gather:
        s_z, r_z, s_x, r_x, s_c, r_c = rest[23:29]
        rows = win.shape[0]
        total = 2 * nw - 1

        def shard(hh, ww):
            return W.at[pl.ds(pl.multiple_of((hh * nw + ww) * rows, 16), rows), :]

        def column(i):
            if i == 0:
                return w
            k, d = divmod(i - 1, 2)
            return w + 1 + k if d else w - 1 - k

        def held(i):
            if i == 0:
                return w >= 0
            return column(i) < nw if (i - 1) % 2 else column(i) >= 0

        def zc(d, k):
            part = shard(h, w + k if d else w - k)
            return copy(part, part, s_z.at[d, k], r_z.at[d, k], dev["l" if d else "r"])

        def xc(i):
            part = shard(h, column(i))
            return copy(part, part, s_x.at[i], r_x.at[i], xdev)

        def cc(i):
            part = shard(h, column(i)) if i < total else shard(xdev[0], column(i - total))
            return copy(part, part, s_c.at[i], r_c.at[i], cdev)

        W[pl.ds(pl.multiple_of((h * nw + w) * rows, 16), rows), :] = win[...]
        pl.when(right)(lambda: zc(0, 0).start())
        pl.when(left)(lambda: zc(1, 0).start())
        xc(0).start()
        cc(0).start()

    def fill(index):
        shape = kv.at[index].shape[:-1] + (HEAD_DIM,)
        kv[index + (slice(0, HEAD_DIM),)] = jnp.full(shape, ABSENT, BF16)
        kv[index + (slice(HEAD_DIM, 2 * HEAD_DIM),)] = jnp.zeros(shape, BF16)

    every = slice(None)
    for hd in range(heads):
        for c in range(4):
            pl.when(jnp.logical_not(up))(functools.partial(fill, (hd, c, 0, every)))
            pl.when(jnp.logical_not(down))(functools.partial(fill, (hd, c, 2, every)))
        pl.when(jnp.logical_not(left) & up)(functools.partial(fill, (hd, 0, 0, every)))
        pl.when(jnp.logical_not(right) & up)(functools.partial(fill, (hd, 3, 0, every)))
        pl.when(jnp.logical_not(left) & down)(functools.partial(fill, (hd, 0, 2, every)))
        pl.when(jnp.logical_not(right) & down)(functools.partial(fill, (hd, 3, 2, every)))
        pl.when(jnp.logical_not(left))(functools.partial(fill, (hd, 0, 1, every)))
        pl.when(jnp.logical_not(right))(functools.partial(fill, (hd, 3, 1, every)))

    if gather:
        def pass_x(i):
            xc(i).wait_recv()
            cc(total + i).start()

        def step(d, k):
            zc(d, k).wait_recv()
            if k + 1 < nw - 1:
                pl.when(left if d else right)(lambda: zc(d, k + 1).start())
            xc(1 + 2 * k + d).start()
            cc(1 + 2 * k + d).start()

        for k in range(nw - 1):
            for d in range(2):
                pl.when(held(1 + 2 * k + d))(functools.partial(step, d, k))
            for i in ([0] if k == 0 else [2 * k - 1, 2 * k]):
                pl.when(held(i))(functools.partial(pass_x, i))
        for i in (2 * nw - 3, 2 * nw - 2):
            pl.when(held(i))(functools.partial(pass_x, i))
        for i in range(total):
            def done(i=i):
                xc(i).wait_send()
                for j in (i, total + i):
                    cc(j).wait_recv()
                    cc(j).wait_send()
            pl.when(held(i))(done)
        for k in range(nw - 1):
            pl.when(right & (w - k >= 0))(lambda: zc(0, k).wait_send())
            pl.when(left & (w + k < nw))(lambda: zc(1, k).wait_send())

    def tile(hd, c, r):
        return kv.at[hd, c, r]

    def side_copy(hd, side):
        if side == "l":
            return copy(tile(hd, 1, 1), tile(hd, 3, 1), s_h.at[hd, 0], r_h.at[hd, 0], dev["l"])
        if side == "r":
            return copy(tile(hd, 2, 1), tile(hd, 0, 1), s_h.at[hd, 1], r_h.at[hd, 1], dev["r"])
        at, i = (2, 2) if side == "u" else (0, 3)
        return copy(kv.at[hd, pl.ds(1, 2), 1], kv.at[hd, pl.ds(1, 2), at],
                    s_h.at[hd, i], r_h.at[hd, i], dev[side])

    def corner(hd, side, c):
        at, i = (2, 4) if side == "u" else (0, 6)
        i += c // 3
        return copy(tile(hd, c, 1), tile(hd, c, at), s_h.at[hd, i], r_h.at[hd, i], dev[side])

    raw[:, width:] = mm(tok[...], W[:, width : 3 * width])
    absent = vcol[...] == 0
    for hd in range(heads):
        cols = slice(hd * HEAD_DIM, (hd + 1) * HEAD_DIM)
        k_raw = raw[:, width + hd * HEAD_DIM : width + (hd + 1) * HEAD_DIM]
        inv = lax.rsqrt(jnp.mean(k_raw * k_raw, axis=-1, keepdims=True) + EPS)
        kn = jnp.where(absent, ABSENT, k_raw * inv * kg[:, cols]).astype(BF16)
        v = raw[:, 2 * width + hd * HEAD_DIM : 2 * width + (hd + 1) * HEAD_DIM].astype(BF16)
        for j in range(2):
            kv[hd, 1 + j, 1, :, 0:HEAD_DIM] = kn[j * tt : (j + 1) * tt]
            kv[hd, 1 + j, 1, :, HEAD_DIM:] = v[j * tt : (j + 1) * tt]
        for side in "lrud":
            pl.when(there[side])(lambda: side_copy(hd, side).start())

    raw[:, 0:width] = mm(tok[...], W[:, 0:width])
    ga[...] = mm(go[...], W[:, 3 * width : 4 * width]).astype(BF16)
    for hd in range(heads):
        cols = slice(hd * HEAD_DIM, (hd + 1) * HEAD_DIM)
        q_raw = raw[:, cols]
        inv = lax.rsqrt(jnp.mean(q_raw * q_raw, axis=-1, keepdims=True) + EPS)
        qb[:, cols] = (q_raw * inv * qg[:, cols]).astype(BF16)

    def forward(hd, side, c):
        side_copy(hd, "r" if c == 0 else "l").wait_recv()
        for s in "ud":
            pl.when(there[s])(lambda: corner(hd, s, c).start())

    for hd in range(heads):
        pl.when(left)(functools.partial(forward, hd, "l", 0))
        pl.when(right)(functools.partial(forward, hd, "r", 3))

    def back(hd, side):
        i = 0 if side == "u" else 1
        return copy(gs.at[hd, i], gr.at[hd, i], s_g.at[hd, i], r_g.at[hd, i], dev[side])

    def back2(hd, side):
        i = 0 if side == "l" else 1
        return copy(gs2.at[hd, i], gr2.at[hd, i], s_g.at[hd, 2 + i], r_g.at[hd, 2 + i], dev[side])

    win_rows = 9 * tt
    for hd in range(heads):
        cols = slice(hd * HEAD_DIM, (hd + 1) * HEAD_DIM)
        for side, other in (("d", "u"), ("u", "d")):
            def arrived(side=side, other=other):
                side_copy(hd, other).wait_recv()
                pl.when(left)(lambda: corner(hd, other, 0).wait_recv())
                pl.when(right)(lambda: corner(hd, other, 3).wait_recv())
            pl.when(there[side])(arrived)
        keys = kv[hd, :, :, :, 0:HEAD_DIM].reshape(12 * tt, HEAD_DIM).astype(F32)
        out = keys > ABSENT * 0.1
        kc[:, 0:HEAD_DIM] = jnp.where(out, 0.0, keys).astype(BF16)
        kc[:, HEAD_DIM:] = jnp.where(out, -1e9, 0.0).astype(BF16)
        for j in range(2):
            rows_j = slice(j * tt, (j + 1) * tt)
            span = slice(3 * j * tt, 3 * j * tt + win_rows)
            q = qb[rows_j, cols]
            up_ = ga[rows_j, cols]
            both = kc[span, :]
            values = kv[hd, j : j + 3, :, :, HEAD_DIM:].reshape(win_rows, HEAD_DIM)
            s = mm(jnp.concatenate([q, jnp.ones_like(q)], axis=1), both, NT)
            e = jnp.exp2(s * (FACTOR * LOG2E))
            p = e * (1.0 / jnp.sum(e, axis=-1, keepdims=True))
            pb = p.astype(BF16)
            att[rows_j, cols] = mm(pb, values).astype(BF16)
            gp = mm(up_, values, NT)
            ds = (p * (gp - jnp.sum(p * gp, axis=-1, keepdims=True))).astype(BF16)
            gq[rows_j, cols] = mm(ds, both[:, 0:HEAD_DIM]) * FACTOR
            dk = mm(ds, q, TN) * FACTOR
            dv = mm(pb, up_, TN)
            if j == 0:
                gacc[hd, 0:win_rows, 0:HEAD_DIM] = dk
                gacc[hd, 0:win_rows, HEAD_DIM:] = dv
            else:
                lo = 3 * tt
                gacc[hd, lo:win_rows, 0:HEAD_DIM] += dk[: win_rows - lo]
                gacc[hd, lo:win_rows, HEAD_DIM:] += dv[: win_rows - lo]
                gacc[hd, win_rows:, 0:HEAD_DIM] = dk[win_rows - lo :]
                gacc[hd, win_rows:, HEAD_DIM:] = dv[win_rows - lo :]
        for i, side in ((0, "u"), (1, "d")):
            for c in range(4):
                at = (3 * c + 2 * i) * tt
                gs[hd, i, c] = gacc[hd, at : at + tt, :].astype(BF16)
            pl.when(there[side])(lambda: back(hd, side).start())

    half = gin.shape[1]
    other_rows = pl.ds(pl.multiple_of((1 - y) * half, 128), half)
    own_rows = pl.ds(pl.multiple_of(y * half, 128), half)
    m_copy = copy(ms, mr, s_y.at[0], r_y.at[0], peer)
    ms[...] = mm(att[...], W[other_rows, 3 * width : 4 * width], NT).astype(BF16)
    m_copy.start()

    def norm_back(x, gain, g):
        inv = lax.rsqrt(jnp.mean(x * x, axis=-1, keepdims=True) + EPS)
        wg = gain * g
        inner = jnp.mean(wg * x, axis=-1, keepdims=True)
        return (inv * wg - x * (inv * inv * inv) * inner).astype(BF16)

    for hd in range(heads):
        for i, (side, other) in enumerate((("u", "d"), ("d", "u"))):
            def add(i=i, side=side, other=other):
                back(hd, other).wait_recv()
                for c in range(4):
                    at = (3 * c + 1) * tt
                    gacc[hd, at : at + tt, :] += gr[hd, 1 - i, c].astype(F32)
            pl.when(there[side])(add)
        for i, (side, c) in enumerate((("l", 0), ("r", 3))):
            def send(i=i, side=side, c=c):
                at = (3 * c + 1) * tt
                gs2[hd, i] = gacc[hd, at : at + tt, :].astype(BF16)
                back2(hd, side).start()
            pl.when(there[side])(send)

    own_mixed = mm(att[...], W[own_rows, 3 * width : 4 * width], NT).astype(BF16).astype(F32)
    for hd in range(heads):
        cols = slice(hd * HEAD_DIM, (hd + 1) * HEAD_DIM)
        gqkv[:, cols] = norm_back(raw[:, cols], qg[:, cols], gq[:, cols])
    m_copy.wait_recv()
    mixed[...] = (own_mixed + mr[...].astype(F32)).astype(BF16)

    for hd in range(heads):
        for i, (side, other, c) in enumerate((("l", "r", 1), ("r", "l", 2))):
            def add2(i=i, other=other, c=c):
                back2(hd, other).wait_recv()
                at = (3 * c + 1) * tt
                gacc[hd, at : at + tt, :] += gr2[hd, 1 - i].astype(F32)
            pl.when(there[side])(add2)
        cols = slice(hd * HEAD_DIM, (hd + 1) * HEAD_DIM)
        kcols = slice(width + hd * HEAD_DIM, width + (hd + 1) * HEAD_DIM)
        vcols = slice(2 * width + hd * HEAD_DIM, 2 * width + (hd + 1) * HEAD_DIM)
        for j in range(2):
            rows_j = slice(j * tt, (j + 1) * tt)
            at = (3 * (1 + j) + 1) * tt
            gqkv[rows_j, kcols] = norm_back(
                raw[rows_j, kcols], kg[:, cols], gacc[hd, at : at + tt, 0:HEAD_DIM])
            gqkv[rows_j, vcols] = gacc[hd, at : at + tt, HEAD_DIM:].astype(BF16)

    def in_copy(j):
        return copy(ss.at[j], sr.at[j], s_y.at[1 + j], r_y.at[1 + j], peer)

    for j in range(2):
        rows_j = slice(j * tt, (j + 1) * tt)
        ss[j] = mm(gqkv[rows_j, :], W[other_rows, 0 : 3 * width], NT).astype(BF16)
        in_copy(j).start()
    own_in = mm(gqkv[...], W[own_rows, 0 : 3 * width], NT).astype(BF16).astype(F32)
    for j in range(2):
        rows_j = slice(j * tt, (j + 1) * tt)
        in_copy(j).wait_recv()
        gin[rows_j, :] = (own_in[rows_j] + sr[j].astype(F32)).astype(BF16)

    m_copy.wait_send()
    for j in range(2):
        in_copy(j).wait_send()
    for hd in range(heads):
        for side in "lrud":
            pl.when(there[side])(lambda: side_copy(hd, side).wait_send())
        for s in "ud":
            pl.when(there[s] & left)(lambda: corner(hd, s, 0).wait_send())
            pl.when(there[s] & right)(lambda: corner(hd, s, 3).wait_send())
            pl.when(there[s])(lambda: back(hd, s).wait_send())
        for s in "lr":
            pl.when(there[s])(lambda: back2(hd, s).wait_send())


def on_device(nh, nw, tokens, grad_out, qkv_weight, out_weight, q_gain, k_gain, key_valid):
    tile_rows, tile_cols, tt, model = tokens.shape
    count = tile_rows * tile_cols * tt
    width = q_gain.shape[0]
    heads = width // HEAD_DIM
    weights = jnp.concatenate(
        [qkv_weight.reshape(qkv_weight.shape[0], 3 * width), out_weight], axis=1)
    gather = nh == 4 and nw > 1 and weights.shape[0] % 16 == 0
    if not gather:
        weights = lax.all_gather(weights, ("height", "width"), axis=0, tiled=True)
    vcol = jnp.broadcast_to(key_valid.astype(F32).reshape(count, 1), (count, HEAD_DIM))
    half = model // 2
    vm = pltpu.VMEM
    dma = pltpu.SemaphoreType.DMA
    scratch = [vm((model, 4 * width), BF16)] if gather else []
    scratch += [
        vm((count, 3 * width), F32),
        vm((count, width), BF16),
        vm((count, width), BF16),
        vm((heads, 4, 3, tt, 2 * HEAD_DIM), BF16),
        vm((12 * tt, 2 * HEAD_DIM), BF16),
        vm((heads, 12 * tt, 2 * HEAD_DIM), F32),
        vm((count, width), BF16),
        vm((count, width), F32),
        vm((heads, 2, 4, tt, 2 * HEAD_DIM), BF16),
        vm((heads, 2, 4, tt, 2 * HEAD_DIM), BF16),
        vm((heads, 2, tt, 2 * HEAD_DIM), BF16),
        vm((heads, 2, tt, 2 * HEAD_DIM), BF16),
        vm((count, 3 * width), BF16),
        vm((count, half), BF16),
        vm((count, half), BF16),
        vm((2, tt, half), BF16),
        vm((2, tt, half), BF16),
        dma((heads, 8)), dma((heads, 8)),
        dma((heads, 4)), dma((heads, 4)),
        dma((3,)), dma((3,)),
    ]
    if gather:
        n = 2 * nw - 1
        scratch += [dma((2, nw - 1)), dma((2, nw - 1)), dma((n,)), dma((n,)),
                    dma((2 * n,)), dma((2 * n,))]
    mixed, grad_in = pl.pallas_call(
        functools.partial(body, (nh, nw, heads, tt, gather)),
        out_shape=[jax.ShapeDtypeStruct((count, half), BF16)] * 2,
        in_specs=[pl.BlockSpec(memory_space=pltpu.VMEM)] * 6,
        out_specs=[pl.BlockSpec(memory_space=pltpu.VMEM)] * 2,
        scratch_shapes=scratch,
        compiler_params=pltpu.CompilerParams(
            collective_id=0, has_side_effects=True, vmem_limit_bytes=56 * 1024 * 1024),
    )(tokens.reshape(count, model), grad_out.reshape(count, model), weights,
      q_gain.reshape(1, width), k_gain.reshape(1, width), vcol)
    shape = (tile_rows, tile_cols, tt, half)
    return mixed.reshape(shape), grad_in.reshape(shape)


def solution(mesh):
    placed = (
        P("height", "width", None, None),
        P("height", "width", None, None),
        P(("height", "width"), None, "head"),
        P(("height", "width"), "head"),
        P("head"),
        P("head"),
        P("height", "width", None),
    )
    return jax.shard_map(
        functools.partial(on_device, mesh.shape["height"], mesh.shape["width"]),
        mesh=mesh,
        in_specs=placed,
        out_specs=(P("height", "width", None, "head"), P("height", "width", None, "head")),
        check_vma=False,
    )
```

time: 235 us -> 86.9 us (0.37)
  waiting for transfers between devices: 97.9 us -> 0 us
  Pallas kernels: 0 us -> 78 us
  starting transfers between devices: 55.5 us -> 0 us
  matrix products: 27.7 us -> 0 us
  other arithmetic: 22.3 us -> 0.74 us
  between operations: 14.7 us -> 0.67 us
  local copies, waits for them, and re-layouts: 14.5 us -> 6.51 us
    pallas_call x0 -> x1, Pallas kernels: none -> 78 us  [on_device(): pl.pallas_call(functools.partial(body, (nh, nw, heads, tt, gather)), out_...]
    ppermute x20 -> x0, starting transfers between devices: 55.3 us -> none  [the longest x10 29.6 us: padded(): before = lax.ppermute(last, axis, up)]
    all_gather x2 -> x0, waiting for transfers between devices: 54.9 us -> none  [the longest x1 33.9 us: on_device(): lax.all_gather(qkv_weight, ('height', 'width'), axis=0, tiled=True)]
    ppermute x20 -> x0, waiting for transfers between devices: 24.3 us -> none  [the longest x10 18.2 us: padded(): after = lax.ppermute(first, axis, down)]
    dot_general x9 -> x0, matrix products: 20.6 us -> none  [the longest x1 3.37 us: attend(): jnp.einsum('bhqk,bkhe->bqhe', attn_weights, win_values, preferred_element...]
    reduce_scatter x2 -> x0, waiting for transfers between devices: 18 us -> none  [the longest x1 17.9 us: on_device(): lax.psum_scatter(grad_part.astype(jnp.bfloat16), 'head', scatter_dimensio...]
    scatter-add x16 -> x0, other arithmetic: 7.91 us -> none  [fold_windows(): total.at[row_step:row_step + tile_rows, col_step:col_step + tile_cols]]
    div x1 -> x0, matrix products: 7.09 us -> none  [attend(): attn_probs = weights / jnp.sum(weights, axis=-1, keepdims=True)]
  transfers between devices with their start and end apart: 24 -> 0, of which waited for: 10 -> 0; matrix products, arithmetic and copies ran while one was open for 17% -> 0% of each run, Pallas kernels for 0% -> 0%
where the time goes in v1:
time: 86.9 us; the launch traced here: 86 us
  Pallas kernels  78 us (90%)
  local copies, waits for them, and re-layouts  6.51 us (7%)
    pallas_call x1, Pallas kernels, on_device(): pl.pallas_call(functools.partial(body, (nh, nw, heads, tt, gather)), out_...  78 us
    unnamed x12, local copies, waits for them, and re-layouts  3.5 us

profile of v1, /device:TPU:9, one launch (start us, length us, event | category | flops | bytes accessed | tf_op | source)
XLA Modules:
  0.0 86.0 jit_solution(10941634534112420274)
XLA Ops:
  0.6 0.0 copy-start.2
  0.6 0.7 copy-done.2
  1.3 0.0 copy-start.3
  1.3 0.6 reshape.30.refs_3_
  1.9 0.1 copy-done.3
  2.0 0.0 copy-start.4
  2.0 0.6 reshape.31.refs_4_
  2.6 0.1 copy-done.4
  2.7 0.1 broadcast_in_dim.7
  2.8 0.8 broadcast_in_dim.8.refs_5_
  3.5 0.0 copy-start.1
  3.5 1.0 %copy.11 = bf16[3,12,8,384]{3,2,0,1:T(8,128)(2,1)S(1)} copy(bf16[3,12,8,384]{3,2,1,0:T(8,128)(2,1)} %bitcast.11) | data formatting | bytes 442368 | tf_op jit(solution)/shard_map/reshape | solution.py:332
  4.5 0.0 copy-done.1
  4.5 0.7 pad_maximum_fusion.refs_2_
  5.3 78.0 %shard_map.86 = (bf16[288,768]{1,0:T(8,128)(2,1)}, bf16[288,768]{1,0:T(8,128)(2,1)}) custom-call(bf16[288,1536]{1,0:T(8,128)(2,1)} %bitcast.6, bf16[288,1536]{1,0:T(8,128)(2,1)} %bitcast.7, bf16[96,1536]{1,0:T(8,128)(2,1)} %pad_maximum_fusion.refs_2_, f32[1,384]{1,0:T(1,128)} %reshape.30.refs_3_, f32[1,384]{1,0:T(1,128)} %reshape.31.refs_4_, ...), custom_call_target="tpu_custom_call" | custom-call | tf_op jit(solution)/shard_map/pallas_call | solution.py:367
  83.3 0.0 copy-start
  83.3 1.9 %copy.14 = bf16[1,2,144,768]{3,2,1,0:T(8,128)(2,1)} copy(bf16[1,2,144,768]{3,2,1,0:T(8,128)(2,1)} %bitcast.10) | data formatting | bytes 884736
  85.2 0.0 copy-done
  85.2 0.8 copy.15
  (1 shorter events, 0.0 us)
Async XLA Ops:
  0.6 0.7 copy-start.2
  1.3 0.7 copy-start.3
  2.0 0.7 copy-start.4
  3.5 1.0 %copy-start.1 = (bf16[96,384]{1,0:T(8,128)(2,1)S(1)}, bf16[96,384]{1,0:T(8,128)(2,1)}, u32[]{:S(2)}) copy-start(bf16[96,384]{1,0:T(8,128)(2,1)} %param.10) | copy-start | bytes 221188
  83.3 1.9 %copy-start = (bf16[288,768]{1,0:T(8,128)(2,1)S(1)}, bf16[288,768]{1,0:T(8,128)(2,1)}, u32[]{:S(2)}) copy-start(bf16[288,768]{1,0:T(8,128)(2,1)} %get-tuple-element.5) | copy-start | bytes 1327108

commit v2 on v1

--- a/solution.py
+++ b/solution.py
@@ -24,11 +24,19 @@
 
 def body(cfg, *refs):
     nh, nw, heads, tt, gather = cfg
-    tok, go, win, qg, kg, vcol, mixed, gin = refs[:8]
-    rest = list(refs[8:])
+    tok_in, go_in, gains, vcol = refs[:4]
+    win = refs[4]
+    rest = list(refs[6:] if gather else refs[5:])
+    mixed, gin = rest[:2]
+    rest = rest[2:]
     W = rest.pop(0) if gather else win
-    (raw, ga, qb, kv, kc, gacc, att, gq, gs, gr, gs2, gr2, gqkv, ms, mr, ss, sr) = rest[:17]
-    (s_h, r_h, s_g, r_g, s_y, r_y) = rest[17:23]
+    (raw, ga, qb, kv, kc, gacc, att, gq, gs, gr, gs2, gr2, gqkv, atto, gqkvo, Wo, tok, go) = rest[:18]
+    (s_h, r_h, s_g, r_g, s_y, r_y, s_w, r_w, s_in) = rest[18:27]
+    tok_copy = pltpu.make_async_copy(tok_in, tok, s_in.at[0])
+    go_copy = pltpu.make_async_copy(go_in, go, s_in.at[1])
+    tok_copy.start()
+    go_copy.start()
+    qg, kg = gains.at[0:1], gains.at[1:2]
     width = heads * HEAD_DIM
     h, w, y = lax.axis_index("height"), lax.axis_index("width"), lax.axis_index("head")
     up, down, left, right = h > 0, h < nh - 1, w > 0, w < nw - 1
@@ -60,7 +68,7 @@
     pl.semaphore_wait(barrier, count)
 
     if gather:
-        s_z, r_z, s_x, r_x, s_c, r_c = rest[23:29]
+        s_z, r_z, s_x, r_x, s_c, r_c, s_v, r_v = rest[27:35]
         rows = win.shape[0]
         total = 2 * nw - 1
 
@@ -90,11 +98,30 @@
             part = shard(h, column(i)) if i < total else shard(xdev[0], column(i - total))
             return copy(part, part, s_c.at[i], r_c.at[i], cdev)
 
-        W[pl.ds(pl.multiple_of((h * nw + w) * rows, 16), rows), :] = win[...]
+        core = lax.rem(h, 2)
+        mine = h // 2 == 1 - y
+
+        def yc(i):
+            to = Wo.at[pl.ds(pl.multiple_of((core * nw + column(i)) * rows, 16), rows), :]
+            return copy(shard(2 * (1 - y) + core, column(i)), to, s_w.at[i], r_w.at[i], peer)
+
+        def yv(i):
+            part = Wo.at[pl.ds(pl.multiple_of((core * nw + column(i)) * rows, 16), rows), :]
+            return copy(part, part, s_v.at[i], r_v.at[i], cdev)
+
+        own_slot = pl.ds(pl.multiple_of((h * nw + w) * rows, 16), rows)
+        W[own_slot, 0 : 3 * width] = win[...]
+        W[own_slot, 3 * width : 4 * width] = refs[5][...]
         pl.when(right)(lambda: zc(0, 0).start())
         pl.when(left)(lambda: zc(1, 0).start())
         xc(0).start()
         cc(0).start()
+        pl.when(mine)(lambda: yc(0).start())
+    else:
+        half_w = Wo.shape[0]
+        w_copy = copy(win.at[pl.ds(pl.multiple_of((1 - y) * half_w, 16), half_w), :], Wo,
+                      s_w.at[0], r_w.at[0], peer)
+        w_copy.start()
 
     def fill(index):
         shape = kv.at[index].shape[:-1] + (HEAD_DIM,)
@@ -117,6 +144,7 @@
         def pass_x(i):
             xc(i).wait_recv()
             cc(total + i).start()
+            pl.when(jnp.logical_not(mine))(lambda: yc(i).start())
 
         def step(d, k):
             zc(d, k).wait_recv()
@@ -124,6 +152,7 @@
                 pl.when(left if d else right)(lambda: zc(d, k + 1).start())
             xc(1 + 2 * k + d).start()
             cc(1 + 2 * k + d).start()
+            pl.when(mine)(lambda: yc(1 + 2 * k + d).start())
 
         for k in range(nw - 1):
             for d in range(2):
@@ -160,6 +189,11 @@
         i += c // 3
         return copy(tile(hd, c, 1), tile(hd, c, at), s_h.at[hd, i], r_h.at[hd, i], dev[side])
 
+    def sides(hd):
+        for side in "lrud":
+            pl.when(there[side])(lambda: side_copy(hd, side).start())
+
+    tok_copy.wait()
     raw[:, width:] = mm(tok[...], W[:, width : 3 * width])
     absent = vcol[...] == 0
     for hd in range(heads):
@@ -171,9 +205,10 @@
         for j in range(2):
             kv[hd, 1 + j, 1, :, 0:HEAD_DIM] = kn[j * tt : (j + 1) * tt]
             kv[hd, 1 + j, 1, :, HEAD_DIM:] = v[j * tt : (j + 1) * tt]
-        for side in "lrud":
-            pl.when(there[side])(lambda: side_copy(hd, side).start())
-
+        if hd < 2:
+            sides(hd)
+
+    go_copy.wait()
     raw[:, 0:width] = mm(tok[...], W[:, 0:width])
     ga[...] = mm(go[...], W[:, 3 * width : 4 * width]).astype(BF16)
     for hd in range(heads):
@@ -187,9 +222,27 @@
         for s in "ud":
             pl.when(there[s])(lambda: corner(hd, s, c).start())
 
-    for hd in range(heads):
+    def corners(hd):
         pl.when(left)(functools.partial(forward, hd, "l", 0))
         pl.when(right)(functools.partial(forward, hd, "r", 3))
+
+    corners(0)
+    for hd in range(2, heads):
+        sides(hd)
+
+    def to_peer(part, hd):
+        i = part * heads + hd
+        if part == 0:
+            at = (slice(None), pl.ds(hd * HEAD_DIM, HEAD_DIM))
+            return copy(att.at[at], atto.at[at], s_y.at[i], r_y.at[i], peer)
+        at = (slice(None), pl.ds((part - 1) * width + hd * HEAD_DIM, HEAD_DIM))
+        return copy(gqkv.at[at], gqkvo.at[at], s_y.at[i], r_y.at[i], peer)
+
+    def norm_back(x, gain, g):
+        inv = lax.rsqrt(jnp.mean(x * x, axis=-1, keepdims=True) + EPS)
+        wg = gain * g
+        inner = jnp.mean(wg * x, axis=-1, keepdims=True)
+        return (inv * wg - x * (inv * inv * inv) * inner).astype(BF16)
 
     def back(hd, side):
         i = 0 if side == "u" else 1
@@ -202,6 +255,8 @@
     win_rows = 9 * tt
     for hd in range(heads):
         cols = slice(hd * HEAD_DIM, (hd + 1) * HEAD_DIM)
+        if hd + 1 < heads:
+            corners(hd + 1)
         for side, other in (("d", "u"), ("u", "d")):
             def arrived(side=side, other=other):
                 side_copy(hd, other).wait_recv()
@@ -243,19 +298,19 @@
                 at = (3 * c + 2 * i) * tt
                 gs[hd, i, c] = gacc[hd, at : at + tt, :].astype(BF16)
             pl.when(there[side])(lambda: back(hd, side).start())
+        to_peer(0, hd).start()
+        gqkv[:, cols] = norm_back(raw[:, cols], qg[:, cols], gq[:, cols])
+        to_peer(1, hd).start()
 
     half = gin.shape[1]
-    other_rows = pl.ds(pl.multiple_of((1 - y) * half, 128), half)
     own_rows = pl.ds(pl.multiple_of(y * half, 128), half)
-    m_copy = copy(ms, mr, s_y.at[0], r_y.at[0], peer)
-    ms[...] = mm(att[...], W[other_rows, 3 * width : 4 * width], NT).astype(BF16)
-    m_copy.start()
-
-    def norm_back(x, gain, g):
-        inv = lax.rsqrt(jnp.mean(x * x, axis=-1, keepdims=True) + EPS)
-        wg = gain * g
-        inner = jnp.mean(wg * x, axis=-1, keepdims=True)
-        return (inv * wg - x * (inv * inv * inv) * inner).astype(BF16)
+    if gather:
+        def pass_w(i):
+            yc(i).wait_recv()
+            yv(i).start()
+
+        for i in range(total):
+            pl.when(held(i))(functools.partial(pass_w, i))
 
     for hd in range(heads):
         for i, (side, other) in enumerate((("u", "d"), ("d", "u"))):
@@ -272,12 +327,21 @@
                 back2(hd, side).start()
             pl.when(there[side])(send)
 
-    own_mixed = mm(att[...], W[own_rows, 3 * width : 4 * width], NT).astype(BF16).astype(F32)
-    for hd in range(heads):
-        cols = slice(hd * HEAD_DIM, (hd + 1) * HEAD_DIM)
-        gqkv[:, cols] = norm_back(raw[:, cols], qg[:, cols], gq[:, cols])
-    m_copy.wait_recv()
-    mixed[...] = (own_mixed + mr[...].astype(F32)).astype(BF16)
+    out_cols = slice(3 * width, 4 * width)
+    own_mixed = mm(att[...], W[own_rows, out_cols], NT)
+    if gather:
+        def weights_in(i):
+            yv(i).wait_recv()
+            yv(i).wait_send()
+            yc(i).wait_send()
+
+        for i in range(total):
+            pl.when(held(i))(functools.partial(weights_in, i))
+    else:
+        w_copy.wait_recv()
+    for hd in range(heads):
+        to_peer(0, hd).wait_recv()
+    mixed[...] = (own_mixed + mm(atto[...], Wo[:, out_cols], NT)).astype(BF16)
 
     for hd in range(heads):
         for i, (side, other, c) in enumerate((("l", "r", 1), ("r", "l", 2))):
@@ -295,24 +359,30 @@
             gqkv[rows_j, kcols] = norm_back(
                 raw[rows_j, kcols], kg[:, cols], gacc[hd, at : at + tt, 0:HEAD_DIM])
             gqkv[rows_j, vcols] = gacc[hd, at : at + tt, HEAD_DIM:].astype(BF16)
-
-    def in_copy(j):
-        return copy(ss.at[j], sr.at[j], s_y.at[1 + j], r_y.at[1 + j], peer)
-
-    for j in range(2):
-        rows_j = slice(j * tt, (j + 1) * tt)
-        ss[j] = mm(gqkv[rows_j, :], W[other_rows, 0 : 3 * width], NT).astype(BF16)
-        in_copy(j).start()
-    own_in = mm(gqkv[...], W[own_rows, 0 : 3 * width], NT).astype(BF16).astype(F32)
-    for j in range(2):
-        rows_j = slice(j * tt, (j + 1) * tt)
-        in_copy(j).wait_recv()
-        gin[rows_j, :] = (own_in[rows_j] + sr[j].astype(F32)).astype(BF16)
-
-    m_copy.wait_send()
-    for j in range(2):
-        in_copy(j).wait_send()
-    for hd in range(heads):
+        to_peer(2, hd).start()
+        to_peer(3, hd).start()
+
+    for hd in range(heads):
+        to_peer(1, hd).wait_recv()
+        if hd + 1 < heads:
+            to_peer(2, hd).wait_recv()
+            to_peer(3, hd).wait_recv()
+    early = (slice(0, 2 * width - HEAD_DIM), slice(2 * width, 3 * width - HEAD_DIM))
+    late = (slice(2 * width - HEAD_DIM, 2 * width), slice(3 * width - HEAD_DIM, 3 * width))
+    total_in = mm(gqkv[...], W[own_rows, 0 : 3 * width], NT)
+    for part in early:
+        total_in += mm(gqkvo[:, part], Wo[:, part], NT)
+    to_peer(2, heads - 1).wait_recv()
+    to_peer(3, heads - 1).wait_recv()
+    for part in late:
+        total_in += mm(gqkvo[:, part], Wo[:, part], NT)
+    gin[...] = total_in.astype(BF16)
+
+    if not gather:
+        w_copy.wait_send()
+    for hd in range(heads):
+        for part in range(4):
+            to_peer(part, hd).wait_send()
         for side in "lrud":
             pl.when(there[side])(lambda: side_copy(hd, side).wait_send())
         for s in "ud":
@@ -328,11 +398,11 @@
     count = tile_rows * tile_cols * tt
     width = q_gain.shape[0]
     heads = width // HEAD_DIM
-    weights = jnp.concatenate(
-        [qkv_weight.reshape(qkv_weight.shape[0], 3 * width), out_weight], axis=1)
-    gather = nh == 4 and nw > 1 and weights.shape[0] % 16 == 0
+    weights = [qkv_weight.reshape(qkv_weight.shape[0], 3 * width), out_weight]
+    gather = nh == 4 and nw > 1 and out_weight.shape[0] % 16 == 0
     if not gather:
-        weights = lax.all_gather(weights, ("height", "width"), axis=0, tiled=True)
+        whole = jnp.concatenate(weights, axis=1)
+        weights = [lax.all_gather(whole, ("height", "width"), axis=0, tiled=True)]
     vcol = jnp.broadcast_to(key_valid.astype(F32).reshape(count, 1), (count, HEAD_DIM))
     half = model // 2
     vm = pltpu.VMEM
@@ -352,28 +422,32 @@
         vm((heads, 2, tt, 2 * HEAD_DIM), BF16),
         vm((heads, 2, tt, 2 * HEAD_DIM), BF16),
         vm((count, 3 * width), BF16),
-        vm((count, half), BF16),
-        vm((count, half), BF16),
-        vm((2, tt, half), BF16),
-        vm((2, tt, half), BF16),
+        vm((count, width), BF16),
+        vm((count, 3 * width), BF16),
+        vm((half, 4 * width), BF16),
+        vm((count, model), BF16),
+        vm((count, model), BF16),
         dma((heads, 8)), dma((heads, 8)),
         dma((heads, 4)), dma((heads, 4)),
-        dma((3,)), dma((3,)),
+        dma((4 * heads,)), dma((4 * heads,)),
+        dma((2 * nw - 1,)), dma((2 * nw - 1,)),
+        dma((2,)),
     ]
     if gather:
         n = 2 * nw - 1
         scratch += [dma((2, nw - 1)), dma((2, nw - 1)), dma((n,)), dma((n,)),
-                    dma((2 * n,)), dma((2 * n,))]
+                    dma((2 * n,)), dma((2 * n,)), dma((n,)), dma((n,))]
     mixed, grad_in = pl.pallas_call(
         functools.partial(body, (nh, nw, heads, tt, gather)),
         out_shape=[jax.ShapeDtypeStruct((count, half), BF16)] * 2,
-        in_specs=[pl.BlockSpec(memory_space=pltpu.VMEM)] * 6,
+        in_specs=[pl.BlockSpec(memory_space=pl.ANY)] * 2
+        + [pl.BlockSpec(memory_space=pltpu.VMEM)] * (2 + len(weights)),
         out_specs=[pl.BlockSpec(memory_space=pltpu.VMEM)] * 2,
         scratch_shapes=scratch,
         compiler_params=pltpu.CompilerParams(
             collective_id=0, has_side_effects=True, vmem_limit_bytes=56 * 1024 * 1024),
-    )(tokens.reshape(count, model), grad_out.reshape(count, model), weights,
-      q_gain.reshape(1, width), k_gain.reshape(1, width), vcol)
+    )(tokens.reshape(count, model), grad_out.reshape(count, model),
+      jnp.stack([q_gain, k_gain]), vcol, *weights)
     shape = (tile_rows, tile_cols, tt, half)
     return mixed.reshape(shape), grad_in.reshape(shape)
 

time: 86.9 us -> 83.9 us (0.965)
  Pallas kernels: 78 us -> 74.9 us
    pallas_call x1, Pallas kernels: 78 us -> 74.9 us  [on_device(): pl.pallas_call(functools.partial(body, (nh, nw, heads, tt, gather)), out_...]
    unnamed x12 -> x10, local copies, waits for them, and re-layouts: 3.5 us -> 4.06 us
    reshape x3 -> x1, local copies, waits for them, and re-layouts: 2.16 us -> 1.64 us  [on_device(): weights = [qkv_weight.reshape(qkv_weight.shape[0], 3 * width), out_weight]]
where the time goes in v2:
time: 83.9 us; the launch traced here: 82.7 us
  Pallas kernels  74.9 us (89%)
  local copies, waits for them, and re-layouts  6.57 us (8%)
    pallas_call x1, Pallas kernels, on_device(): pl.pallas_call(functools.partial(body, (nh, nw, heads, tt, gather)), out_...  74.9 us
    unnamed x10, local copies, waits for them, and re-layouts  4.06 us

profile of v2, /device:TPU:9, one launch (start us, length us, event | category | flops | bytes accessed | tf_op | source)
XLA Modules:
  0.0 82.7 jit_solution(16118797670772757910)
XLA Ops:
  0.6 0.0 copy-start.1
  0.6 0.7 copy-done.1
  1.3 0.0 copy-start.2
  1.3 0.7 copy-done.2
  2.0 0.0 copy-start.3
  2.0 0.6 pad_maximum_fusion.refs_2_
  2.6 0.1 copy-done.3
  2.7 0.1 broadcast_in_dim.7
  2.8 0.8 broadcast_in_dim.8.refs_3_
  3.5 1.6 %copy.11 = bf16[3,12,8,384]{3,2,0,1:T(8,128)(2,1)} copy(bf16[3,12,8,384]{3,2,1,0:T(8,128)(2,1)} %bitcast.11) | data formatting | bytes 442368 | tf_op jit(solution)/shard_map/reshape | solution.py:401
  5.2 74.9 %shard_map.86 = (bf16[288,768]{1,0:T(8,128)(2,1)}, bf16[288,768]{1,0:T(8,128)(2,1)}) custom-call(bf16[288,1536]{1,0:T(8,128)(2,1)} %bitcast.7, bf16[288,1536]{1,0:T(8,128)(2,1)} %bitcast.8, f32[2,384]{1,0:T(2,128)} %pad_maximum_fusion.refs_2_, f32[288,128]{1,0:T(8,128)} %broadcast_in_dim.8.refs_3_, bf16[96,1152]{1,0:T(8,128)(2,1)} %bitcast.6, ...), custom_call_target="tpu_custom_call" | custom-call | tf_op jit(solution)/shard_map/pallas_call | solution.py:440
  80.1 0.0 copy-start
  80.1 1.9 %copy.14 = bf16[1,2,144,768]{3,2,1,0:T(8,128)(2,1)} copy(bf16[1,2,144,768]{3,2,1,0:T(8,128)(2,1)} %bitcast.10) | data formatting | bytes 884736
  81.9 0.0 copy-done
  81.9 0.8 copy.15
  (3 shorter events, 0.0 us)
Async XLA Ops:
  0.6 0.7 copy-start.1
  1.3 0.7 copy-start.2
  2.0 0.7 copy-start.3
  80.1 1.9 %copy-start = (bf16[288,768]{1,0:T(8,128)(2,1)S(1)}, bf16[288,768]{1,0:T(8,128)(2,1)}, u32[]{:S(2)}) copy-start(bf16[288,768]{1,0:T(8,128)(2,1)} %get-tuple-element.5) | copy-start | bytes 1327108

commit v3 on v2

--- a/solution.py
+++ b/solution.py
@@ -72,8 +72,11 @@
         rows = win.shape[0]
         total = 2 * nw - 1
 
-        def shard(hh, ww):
-            return W.at[pl.ds(pl.multiple_of((hh * nw + ww) * rows, 16), rows), :]
+        def shard(hh, ww, part=None):
+            at = pl.ds(pl.multiple_of((hh * nw + ww) * rows, 16), rows)
+            if part is None:
+                return W.at[at, :]
+            return W.at[at, pl.ds(2 * width * part, 2 * width)]
 
         def column(i):
             if i == 0:
@@ -86,17 +89,18 @@
                 return w >= 0
             return column(i) < nw if (i - 1) % 2 else column(i) >= 0
 
-        def zc(d, k):
-            part = shard(h, w + k if d else w - k)
-            return copy(part, part, s_z.at[d, k], r_z.at[d, k], dev["l" if d else "r"])
-
-        def xc(i):
-            part = shard(h, column(i))
-            return copy(part, part, s_x.at[i], r_x.at[i], xdev)
-
-        def cc(i):
-            part = shard(h, column(i)) if i < total else shard(xdev[0], column(i - total))
-            return copy(part, part, s_c.at[i], r_c.at[i], cdev)
+        def zc(p, d, k):
+            part = shard(h, w + k if d else w - k, p)
+            return copy(part, part, s_z.at[p, d, k], r_z.at[p, d, k], dev["l" if d else "r"])
+
+        def xc(p, i):
+            part = shard(h, column(i), p)
+            return copy(part, part, s_x.at[p, i], r_x.at[p, i], xdev)
+
+        def cc(p, i):
+            hh, i_ = (h, i) if i < total else (xdev[0], i - total)
+            part = shard(hh, column(i_), p)
+            return copy(part, part, s_c.at[p, i], r_c.at[p, i], cdev)
 
         core = lax.rem(h, 2)
         mine = h // 2 == 1 - y
@@ -110,13 +114,64 @@
             return copy(part, part, s_v.at[i], r_v.at[i], cdev)
 
         own_slot = pl.ds(pl.multiple_of((h * nw + w) * rows, 16), rows)
-        W[own_slot, 0 : 3 * width] = win[...]
+        W[own_slot, 0 : 2 * width] = win[:, width : 3 * width]
+        W[own_slot, 2 * width : 3 * width] = win[:, 0:width]
         W[own_slot, 3 * width : 4 * width] = refs[5][...]
-        pl.when(right)(lambda: zc(0, 0).start())
-        pl.when(left)(lambda: zc(1, 0).start())
-        xc(0).start()
-        cc(0).start()
-        pl.when(mine)(lambda: yc(0).start())
+
+        def begin(p):
+            pl.when(right)(lambda: zc(p, 0, 0).start())
+            pl.when(left)(lambda: zc(p, 1, 0).start())
+            xc(p, 0).start()
+            cc(p, 0).start()
+            if p:
+                pl.when(mine)(lambda: yc(0).start())
+
+        def pass_x(p, i):
+            xc(p, i).wait_recv()
+            cc(p, total + i).start()
+            if p:
+                pl.when(jnp.logical_not(mine))(lambda: yc(i).start())
+
+        def step(p, d, k):
+            zc(p, d, k).wait_recv()
+            if k + 1 < nw - 1:
+                pl.when(left if d else right)(lambda: zc(p, d, k + 1).start())
+            i = 1 + 2 * k + d
+            xc(p, i).start()
+            cc(p, i).start()
+            if p:
+                pl.when(mine)(lambda: yc(i).start())
+
+        def stage(p, k):
+            for d in range(2):
+                pl.when(held(1 + 2 * k + d))(functools.partial(step, p, d, k))
+            for i in ([0] if k == 0 else [2 * k - 1, 2 * k]):
+                pl.when(held(i))(functools.partial(pass_x, p, i))
+
+        def finish(p):
+            for i in (2 * nw - 3, 2 * nw - 2):
+                pl.when(held(i))(functools.partial(pass_x, p, i))
+
+            def done(i):
+                cc(p, i).wait_recv()
+                cc(p, total + i).wait_recv()
+
+            for i in range(total):
+                pl.when(held(i))(functools.partial(done, i))
+
+        def sent(p):
+            def done(i):
+                xc(p, i).wait_send()
+                cc(p, i).wait_send()
+                cc(p, total + i).wait_send()
+
+            for i in range(total):
+                pl.when(held(i))(functools.partial(done, i))
+            for k in range(nw - 1):
+                pl.when(right & (w - k >= 0))(lambda: zc(p, 0, k).wait_send())
+                pl.when(left & (w + k < nw))(lambda: zc(p, 1, k).wait_send())
+
+        begin(0)
     else:
         half_w = Wo.shape[0]
         w_copy = copy(win.at[pl.ds(pl.multiple_of((1 - y) * half_w, 16), half_w), :], Wo,
@@ -141,36 +196,10 @@
         pl.when(jnp.logical_not(right))(functools.partial(fill, (hd, 3, 1, every)))
 
     if gather:
-        def pass_x(i):
-            xc(i).wait_recv()
-            cc(total + i).start()
-            pl.when(jnp.logical_not(mine))(lambda: yc(i).start())
-
-        def step(d, k):
-            zc(d, k).wait_recv()
-            if k + 1 < nw - 1:
-                pl.when(left if d else right)(lambda: zc(d, k + 1).start())
-            xc(1 + 2 * k + d).start()
-            cc(1 + 2 * k + d).start()
-            pl.when(mine)(lambda: yc(1 + 2 * k + d).start())
-
         for k in range(nw - 1):
-            for d in range(2):
-                pl.when(held(1 + 2 * k + d))(functools.partial(step, d, k))
-            for i in ([0] if k == 0 else [2 * k - 1, 2 * k]):
-                pl.when(held(i))(functools.partial(pass_x, i))
-        for i in (2 * nw - 3, 2 * nw - 2):
-            pl.when(held(i))(functools.partial(pass_x, i))
-        for i in range(total):
-            def done(i=i):
-                xc(i).wait_send()
-                for j in (i, total + i):
-                    cc(j).wait_recv()
-                    cc(j).wait_send()
-            pl.when(held(i))(done)
-        for k in range(nw - 1):
-            pl.when(right & (w - k >= 0))(lambda: zc(0, k).wait_send())
-            pl.when(left & (w + k < nw))(lambda: zc(1, k).wait_send())
+            stage(0, k)
+        begin(1)
+        finish(0)
 
     def tile(hd, c, r):
         return kv.at[hd, c, r]
@@ -194,29 +223,20 @@
             pl.when(there[side])(lambda: side_copy(hd, side).start())
 
     tok_copy.wait()
-    raw[:, width:] = mm(tok[...], W[:, width : 3 * width])
+    raw[:, 0 : 2 * width] = mm(tok[...], W[:, 0 : 2 * width])
     absent = vcol[...] == 0
     for hd in range(heads):
         cols = slice(hd * HEAD_DIM, (hd + 1) * HEAD_DIM)
-        k_raw = raw[:, width + hd * HEAD_DIM : width + (hd + 1) * HEAD_DIM]
+        k_raw = raw[:, cols]
         inv = lax.rsqrt(jnp.mean(k_raw * k_raw, axis=-1, keepdims=True) + EPS)
         kn = jnp.where(absent, ABSENT, k_raw * inv * kg[:, cols]).astype(BF16)
-        v = raw[:, 2 * width + hd * HEAD_DIM : 2 * width + (hd + 1) * HEAD_DIM].astype(BF16)
+        v = raw[:, width + hd * HEAD_DIM : width + (hd + 1) * HEAD_DIM].astype(BF16)
         for j in range(2):
             kv[hd, 1 + j, 1, :, 0:HEAD_DIM] = kn[j * tt : (j + 1) * tt]
             kv[hd, 1 + j, 1, :, HEAD_DIM:] = v[j * tt : (j + 1) * tt]
         if hd < 2:
             sides(hd)
 
-    go_copy.wait()
-    raw[:, 0:width] = mm(tok[...], W[:, 0:width])
-    ga[...] = mm(go[...], W[:, 3 * width : 4 * width]).astype(BF16)
-    for hd in range(heads):
-        cols = slice(hd * HEAD_DIM, (hd + 1) * HEAD_DIM)
-        q_raw = raw[:, cols]
-        inv = lax.rsqrt(jnp.mean(q_raw * q_raw, axis=-1, keepdims=True) + EPS)
-        qb[:, cols] = (q_raw * inv * qg[:, cols]).astype(BF16)
-
     def forward(hd, side, c):
         side_copy(hd, "r" if c == 0 else "l").wait_recv()
         for s in "ud":
@@ -226,16 +246,32 @@
         pl.when(left)(functools.partial(forward, hd, "l", 0))
         pl.when(right)(functools.partial(forward, hd, "r", 3))
 
-    corners(0)
-    for hd in range(2, heads):
-        sides(hd)
+    for k in range(max(nw - 1, heads)):
+        if gather and k < nw - 1:
+            stage(1, k)
+        if k + 2 < heads:
+            sides(k + 2)
+        if k < heads - 1:
+            corners(k)
+    if gather:
+        finish(1)
+
+    go_copy.wait()
+    raw[:, 2 * width :] = mm(tok[...], W[:, 2 * width : 3 * width])
+    ga[...] = mm(go[...], W[:, 3 * width : 4 * width]).astype(BF16)
+    for hd in range(heads):
+        cols = slice(hd * HEAD_DIM, (hd + 1) * HEAD_DIM)
+        q_raw = raw[:, 2 * width + hd * HEAD_DIM : 2 * width + (hd + 1) * HEAD_DIM]
+        inv = lax.rsqrt(jnp.mean(q_raw * q_raw, axis=-1, keepdims=True) + EPS)
+        qb[:, cols] = (q_raw * inv * qg[:, cols]).astype(BF16)
 
     def to_peer(part, hd):
         i = part * heads + hd
         if part == 0:
             at = (slice(None), pl.ds(hd * HEAD_DIM, HEAD_DIM))
             return copy(att.at[at], atto.at[at], s_y.at[i], r_y.at[i], peer)
-        at = (slice(None), pl.ds((part - 1) * width + hd * HEAD_DIM, HEAD_DIM))
+        base = (2 * width, 0, width)[part - 1]
+        at = (slice(None), pl.ds(base + hd * HEAD_DIM, HEAD_DIM))
         return copy(gqkv.at[at], gqkvo.at[at], s_y.at[i], r_y.at[i], peer)
 
     def norm_back(x, gain, g):
@@ -255,8 +291,8 @@
     win_rows = 9 * tt
     for hd in range(heads):
         cols = slice(hd * HEAD_DIM, (hd + 1) * HEAD_DIM)
-        if hd + 1 < heads:
-            corners(hd + 1)
+        if hd == 0:
+            corners(heads - 1)
         for side, other in (("d", "u"), ("u", "d")):
             def arrived(side=side, other=other):
                 side_copy(hd, other).wait_recv()
@@ -299,7 +335,8 @@
                 gs[hd, i, c] = gacc[hd, at : at + tt, :].astype(BF16)
             pl.when(there[side])(lambda: back(hd, side).start())
         to_peer(0, hd).start()
-        gqkv[:, cols] = norm_back(raw[:, cols], qg[:, cols], gq[:, cols])
+        qcols = slice(2 * width + hd * HEAD_DIM, 2 * width + (hd + 1) * HEAD_DIM)
+        gqkv[:, qcols] = norm_back(raw[:, qcols], qg[:, cols], gq[:, cols])
         to_peer(1, hd).start()
 
     half = gin.shape[1]
@@ -351,8 +388,8 @@
                 gacc[hd, at : at + tt, :] += gr2[hd, 1 - i].astype(F32)
             pl.when(there[side])(add2)
         cols = slice(hd * HEAD_DIM, (hd + 1) * HEAD_DIM)
-        kcols = slice(width + hd * HEAD_DIM, width + (hd + 1) * HEAD_DIM)
-        vcols = slice(2 * width + hd * HEAD_DIM, 2 * width + (hd + 1) * HEAD_DIM)
+        kcols = cols
+        vcols = slice(width + hd * HEAD_DIM, width + (hd + 1) * HEAD_DIM)
         for j in range(2):
             rows_j = slice(j * tt, (j + 1) * tt)
             at = (3 * (1 + j) + 1) * tt
@@ -367,8 +404,9 @@
         if hd + 1 < heads:
             to_peer(2, hd).wait_recv()
             to_peer(3, hd).wait_recv()
-    early = (slice(0, 2 * width - HEAD_DIM), slice(2 * width, 3 * width - HEAD_DIM))
-    late = (slice(2 * width - HEAD_DIM, 2 * width), slice(3 * width - HEAD_DIM, 3 * width))
+    early = (slice(0, width - HEAD_DIM), slice(width, 2 * width - HEAD_DIM),
+             slice(2 * width, 3 * width))
+    late = (slice(width - HEAD_DIM, width), slice(2 * width - HEAD_DIM, 2 * width))
     total_in = mm(gqkv[...], W[own_rows, 0 : 3 * width], NT)
     for part in early:
         total_in += mm(gqkvo[:, part], Wo[:, part], NT)
@@ -378,7 +416,10 @@
         total_in += mm(gqkvo[:, part], Wo[:, part], NT)
     gin[...] = total_in.astype(BF16)
 
-    if not gather:
+    if gather:
+        sent(0)
+        sent(1)
+    else:
         w_copy.wait_send()
     for hd in range(heads):
         for part in range(4):
@@ -401,7 +442,8 @@
     weights = [qkv_weight.reshape(qkv_weight.shape[0], 3 * width), out_weight]
     gather = nh == 4 and nw > 1 and out_weight.shape[0] % 16 == 0
     if not gather:
-        whole = jnp.concatenate(weights, axis=1)
+        ordered = [weights[0][:, width:], weights[0][:, :width], out_weight]
+        whole = jnp.concatenate(ordered, axis=1)
         weights = [lax.all_gather(whole, ("height", "width"), axis=0, tiled=True)]
     vcol = jnp.broadcast_to(key_valid.astype(F32).reshape(count, 1), (count, HEAD_DIM))
     half = model // 2
@@ -435,8 +477,8 @@
     ]
     if gather:
         n = 2 * nw - 1
-        scratch += [dma((2, nw - 1)), dma((2, nw - 1)), dma((n,)), dma((n,)),
-                    dma((2 * n,)), dma((2 * n,)), dma((n,)), dma((n,))]
+        scratch += [dma((2, 2, nw - 1)), dma((2, 2, nw - 1)), dma((2, n)), dma((2, n)),
+                    dma((2, 2 * n)), dma((2, 2 * n)), dma((n,)), dma((n,))]
     mixed, grad_in = pl.pallas_call(
         functools.partial(body, (nh, nw, heads, tt, gather)),
         out_shape=[jax.ShapeDtypeStruct((count, half), BF16)] * 2,

time: 83.9 us -> 86.4 us (1.030)
  the two profiles are of different devices: /device:TPU:9 before, /device:TPU:0 now
where the time goes in v3:
time: 86.4 us; the launch traced here: 86.2 us
  Pallas kernels  78.3 us (91%)
  local copies, waits for them, and re-layouts  6.57 us (8%)
    pallas_call x1, Pallas kernels, on_device(): pl.pallas_call(functools.partial(body, (nh, nw, heads, tt, gather)), out_...  78.3 us
    unnamed x10, local copies, waits for them, and re-layouts  4.06 us

profile of v3, /device:TPU:0, one launch (start us, length us, event | category | flops | bytes accessed | tf_op | source)
XLA Modules:
  0.0 86.2 jit_solution(14044466582434880287)
XLA Ops:
  0.6 0.0 copy-start.1
  0.6 0.7 copy-done.1
  1.3 0.0 copy-start.2
  1.3 0.7 copy-done.2
  2.0 0.0 copy-start.3
  2.0 0.6 pad_maximum_fusion.refs_2_
  2.6 0.1 copy-done.3
  2.7 0.1 broadcast_in_dim.7
  2.8 0.8 broadcast_in_dim.8.refs_3_
  3.5 1.6 %copy.11 = bf16[3,12,8,384]{3,2,0,1:T(8,128)(2,1)} copy(bf16[3,12,8,384]{3,2,1,0:T(8,128)(2,1)} %bitcast.11) | data formatting | bytes 442368 | tf_op jit(solution)/shard_map/reshape | solution.py:442
  5.2 78.3 %shard_map.86 = (bf16[288,768]{1,0:T(8,128)(2,1)}, bf16[288,768]{1,0:T(8,128)(2,1)}) custom-call(bf16[288,1536]{1,0:T(8,128)(2,1)} %bitcast.7, bf16[288,1536]{1,0:T(8,128)(2,1)} %bitcast.8, f32[2,384]{1,0:T(2,128)} %pad_maximum_fusion.refs_2_, f32[288,128]{1,0:T(8,128)} %broadcast_in_dim.8.refs_3_, bf16[96,1152]{1,0:T(8,128)(2,1)} %bitcast.6, ...), custom_call_target="tpu_custom_call" | custom-call | tf_op jit(solution)/shard_map/pallas_call | solution.py:482
  83.5 0.0 copy-start
  83.5 1.9 %copy.14 = bf16[1,2,144,768]{3,2,1,0:T(8,128)(2,1)} copy(bf16[1,2,144,768]{3,2,1,0:T(8,128)(2,1)} %bitcast.10) | data formatting | bytes 884736
  85.4 0.0 copy-done
  85.4 0.8 copy.15
  (3 shorter events, 0.0 us)
Async XLA Ops:
  0.6 0.7 copy-start.1
  1.3 0.7 copy-start.2
  2.0 0.7 copy-start.3
  83.5 1.9 %copy-start = (bf16[288,768]{1,0:T(8,128)(2,1)S(1)}, bf16[288,768]{1,0:T(8,128)(2,1)}, u32[]{:S(2)}) copy-start(bf16[288,768]{1,0:T(8,128)(2,1)} %get-tuple-element.5) | copy-start | bytes 1327108

commit v4 on v2

--- a/solution.py
+++ b/solution.py
@@ -24,9 +24,9 @@
 
 def body(cfg, *refs):
     nh, nw, heads, tt, gather = cfg
-    tok_in, go_in, gains, vcol = refs[:4]
-    win = refs[4]
-    rest = list(refs[6:] if gather else refs[5:])
+    tok_in, go_in, q_gain, k_gain, vcol = refs[:5]
+    win = refs[5]
+    rest = list(refs[7:] if gather else refs[6:])
     mixed, gin = rest[:2]
     rest = rest[2:]
     W = rest.pop(0) if gather else win
@@ -36,7 +36,7 @@
     go_copy = pltpu.make_async_copy(go_in, go, s_in.at[1])
     tok_copy.start()
     go_copy.start()
-    qg, kg = gains.at[0:1], gains.at[1:2]
+    qg, kg = q_gain[...].reshape(1, -1), k_gain[...].reshape(1, -1)
     width = heads * HEAD_DIM
     h, w, y = lax.axis_index("height"), lax.axis_index("width"), lax.axis_index("head")
     up, down, left, right = h > 0, h < nh - 1, w > 0, w < nw - 1
@@ -111,7 +111,7 @@
 
         own_slot = pl.ds(pl.multiple_of((h * nw + w) * rows, 16), rows)
         W[own_slot, 0 : 3 * width] = win[...]
-        W[own_slot, 3 * width : 4 * width] = refs[5][...]
+        W[own_slot, 3 * width : 4 * width] = refs[6][...]
         pl.when(right)(lambda: zc(0, 0).start())
         pl.when(left)(lambda: zc(1, 0).start())
         xc(0).start()
@@ -159,18 +159,33 @@
                 pl.when(held(1 + 2 * k + d))(functools.partial(step, d, k))
             for i in ([0] if k == 0 else [2 * k - 1, 2 * k]):
                 pl.when(held(i))(functools.partial(pass_x, i))
+        def block(hh):
+            at = pl.ds(pl.multiple_of(hh * nw * rows, 128), nw * rows)
+            return mm(tok[:, at], W[at, width : 3 * width])
+
+        tok_copy.wait()
+        raw[:, width:] = block(h)
+        for i in range(total):
+            pl.when(held(i))(lambda: cc(i).wait_recv())
+        raw[:, width:] += block(cdev[0])
         for i in (2 * nw - 3, 2 * nw - 2):
             pl.when(held(i))(functools.partial(pass_x, i))
+        raw[:, width:] += block(xdev[0])
         for i in range(total):
-            def done(i=i):
+            pl.when(held(i))(lambda: cc(total + i).wait_recv())
+        raw[:, width:] += block(lax.rem(cdev[0] + 2, nh))
+
+        def all_sent():
+            def done(i):
                 xc(i).wait_send()
-                for j in (i, total + i):
-                    cc(j).wait_recv()
-                    cc(j).wait_send()
-            pl.when(held(i))(done)
-        for k in range(nw - 1):
-            pl.when(right & (w - k >= 0))(lambda: zc(0, k).wait_send())
-            pl.when(left & (w + k < nw))(lambda: zc(1, k).wait_send())
+                cc(i).wait_send()
+                cc(total + i).wait_send()
+
+            for i in range(total):
+                pl.when(held(i))(functools.partial(done, i))
+            for k in range(nw - 1):
+                pl.when(right & (w - k >= 0))(lambda: zc(0, k).wait_send())
+                pl.when(left & (w + k < nw))(lambda: zc(1, k).wait_send())
 
     def tile(hd, c, r):
         return kv.at[hd, c, r]
@@ -193,8 +208,9 @@
         for side in "lrud":
             pl.when(there[side])(lambda: side_copy(hd, side).start())
 
-    tok_copy.wait()
-    raw[:, width:] = mm(tok[...], W[:, width : 3 * width])
+    if not gather:
+        tok_copy.wait()
+        raw[:, width:] = mm(tok[...], W[:, width : 3 * width])
     absent = vcol[...] == 0
     for hd in range(heads):
         cols = slice(hd * HEAD_DIM, (hd + 1) * HEAD_DIM)
@@ -378,7 +394,9 @@
         total_in += mm(gqkvo[:, part], Wo[:, part], NT)
     gin[...] = total_in.astype(BF16)
 
-    if not gather:
+    if gather:
+        all_sent()
+    else:
         w_copy.wait_send()
     for hd in range(heads):
         for part in range(4):
@@ -399,7 +417,7 @@
     width = q_gain.shape[0]
     heads = width // HEAD_DIM
     weights = [qkv_weight.reshape(qkv_weight.shape[0], 3 * width), out_weight]
-    gather = nh == 4 and nw > 1 and out_weight.shape[0] % 16 == 0
+    gather = nh == 4 and nw > 1 and out_weight.shape[0] % 32 == 0
     if not gather:
         whole = jnp.concatenate(weights, axis=1)
         weights = [lax.all_gather(whole, ("height", "width"), axis=0, tiled=True)]
@@ -441,13 +459,13 @@
         functools.partial(body, (nh, nw, heads, tt, gather)),
         out_shape=[jax.ShapeDtypeStruct((count, half), BF16)] * 2,
         in_specs=[pl.BlockSpec(memory_space=pl.ANY)] * 2
-        + [pl.BlockSpec(memory_space=pltpu.VMEM)] * (2 + len(weights)),
+        + [pl.BlockSpec(memory_space=pltpu.VMEM)] * (3 + len(weights)),
         out_specs=[pl.BlockSpec(memory_space=pltpu.VMEM)] * 2,
         scratch_shapes=scratch,
         compiler_params=pltpu.CompilerParams(
             collective_id=0, has_side_effects=True, vmem_limit_bytes=56 * 1024 * 1024),
     )(tokens.reshape(count, model), grad_out.reshape(count, model),
-      jnp.stack([q_gain, k_gain]), vcol, *weights)
+      q_gain, k_gain, vcol, *weights)
     shape = (tile_rows, tile_cols, tt, half)
     return mixed.reshape(shape), grad_in.reshape(shape)
 

time: 83.9 us -> 81.2 us (0.968); the launches traced: 82.7 us -> 81 us
    unnamed x10 -> x6, local copies, waits for them, and re-layouts: 4.06 us -> 3.3 us
where the time goes in v4:
time: 81.2 us; the launch traced here: 81 us
  Pallas kernels  74.5 us (92%)
  local copies, waits for them, and re-layouts  5.79 us (7%)
    pallas_call x1, Pallas kernels, on_device(): pl.pallas_call(functools.partial(body, (nh, nw, heads, tt, gather)), out_...  74.5 us
    unnamed x6, local copies, waits for them, and re-layouts  3.3 us
    reshape x1, local copies, waits for them, and re-layouts, on_device(): weights = [qkv_weight.reshape(qkv_weight.shape[0], 3 * width), out_weight]  1.64 us

profile of v4, /device:TPU:9, one launch (start us, length us, event | category | flops | bytes accessed | tf_op | source)
XLA Modules:
  0.0 81.0 jit_solution(6266450017234768181)
XLA Ops:
  0.6 0.0 copy-start.1
  0.6 0.7 copy-done.1
  1.3 0.1 broadcast_in_dim.7
  1.4 0.8 broadcast_in_dim.8.refs_4_
  2.2 1.6 %copy.11 = bf16[3,12,8,384]{3,2,0,1:T(8,128)(2,1)} copy(bf16[3,12,8,384]{3,2,1,0:T(8,128)(2,1)} %bitcast.11) | data formatting | bytes 442368 | tf_op jit(solution)/shard_map/reshape | solution.py:419
  3.8 74.5 %shard_map.86 = (bf16[288,768]{1,0:T(8,128)(2,1)}, bf16[288,768]{1,0:T(8,128)(2,1)}) custom-call(bf16[288,1536]{1,0:T(8,128)(2,1)} %bitcast.7, bf16[288,1536]{1,0:T(8,128)(2,1)} %bitcast.8, f32[384]{0:T(512)} %refs_2_.1, f32[384]{0:T(512)} %refs_3_.1, f32[288,128]{1,0:T(8,128)} %broadcast_in_dim.8.refs_4_, bf16[96,1152]{1,0:T(8,128)(2,1)} %bitcast.6, ...), custom_call_target="tpu_custom_call" | custom-call | tf_op jit(solution)/shard_map/pallas_call | solution.py:458
  78.4 0.0 copy-start
  78.4 1.9 %copy.14 = bf16[1,2,144,768]{3,2,1,0:T(8,128)(2,1)} copy(bf16[1,2,144,768]{3,2,1,0:T(8,128)(2,1)} %bitcast.10) | data formatting | bytes 884736
  80.2 0.0 copy-done
  80.2 0.8 copy.15
  (1 shorter events, 0.0 us)
Async XLA Ops:
  0.6 0.7 copy-start.1
  78.4 1.9 %copy-start = (bf16[288,768]{1,0:T(8,128)(2,1)S(1)}, bf16[288,768]{1,0:T(8,128)(2,1)}, u32[]{:S(2)}) copy-start(bf16[288,768]{1,0:T(8,128)(2,1)} %get-tuple-element.5) | copy-start | bytes 1327108

commit v5 on v4

--- a/solution.py
+++ b/solution.py
@@ -359,6 +359,11 @@
         to_peer(0, hd).wait_recv()
     mixed[...] = (own_mixed + mm(atto[...], Wo[:, out_cols], NT)).astype(BF16)
 
+    total_in = mm(gqkv[:, 0:width], W[own_rows, 0:width], NT)
+    for hd in range(heads):
+        to_peer(1, hd).wait_recv()
+    total_in += mm(gqkvo[:, 0:width], Wo[:, 0:width], NT)
+
     for hd in range(heads):
         for i, (side, other, c) in enumerate((("l", "r", 1), ("r", "l", 2))):
             def add2(i=i, other=other, c=c):
@@ -378,14 +383,12 @@
         to_peer(2, hd).start()
         to_peer(3, hd).start()
 
-    for hd in range(heads):
-        to_peer(1, hd).wait_recv()
-        if hd + 1 < heads:
-            to_peer(2, hd).wait_recv()
-            to_peer(3, hd).wait_recv()
-    early = (slice(0, 2 * width - HEAD_DIM), slice(2 * width, 3 * width - HEAD_DIM))
+    total_in += mm(gqkv[:, width:], W[own_rows, width : 3 * width], NT)
+    for hd in range(heads - 1):
+        to_peer(2, hd).wait_recv()
+        to_peer(3, hd).wait_recv()
+    early = (slice(width, 2 * width - HEAD_DIM), slice(2 * width, 3 * width - HEAD_DIM))
     late = (slice(2 * width - HEAD_DIM, 2 * width), slice(3 * width - HEAD_DIM, 3 * width))
-    total_in = mm(gqkv[...], W[own_rows, 0 : 3 * width], NT)
     for part in early:
         total_in += mm(gqkvo[:, part], Wo[:, part], NT)
     to_peer(2, heads - 1).wait_recv()

time: 81.2 us -> 82 us (level)
  no operation moved by 1% of the time
where the time goes in v5:
time: 82 us; the launch traced here: 81.7 us
  Pallas kernels  75.3 us (92%)
  local copies, waits for them, and re-layouts  5.79 us (7%)
    pallas_call x1, Pallas kernels, on_device(): pl.pallas_call(functools.partial(body, (nh, nw, heads, tt, gather)), out_...  75.3 us
    unnamed x6, local copies, waits for them, and re-layouts  3.3 us
    reshape x1, local copies, waits for them, and re-layouts, on_device(): weights = [qkv_weight.reshape(qkv_weight.shape[0], 3 * width), out_weight]  1.64 us

profile of v5, /device:TPU:9, one launch (start us, length us, event | category | flops | bytes accessed | tf_op | source)
XLA Modules:
  0.0 81.7 jit_solution(8761570233348805752)
XLA Ops:
  0.6 0.0 copy-start.1
  0.6 0.7 copy-done.1
  1.3 0.1 broadcast_in_dim.7
  1.4 0.8 broadcast_in_dim.8.refs_4_
  2.2 1.6 %copy.11 = bf16[3,12,8,384]{3,2,0,1:T(8,128)(2,1)} copy(bf16[3,12,8,384]{3,2,1,0:T(8,128)(2,1)} %bitcast.11) | data formatting | bytes 442368 | tf_op jit(solution)/shard_map/reshape | solution.py:422
  3.8 75.3 %shard_map.86 = (bf16[288,768]{1,0:T(8,128)(2,1)}, bf16[288,768]{1,0:T(8,128)(2,1)}) custom-call(bf16[288,1536]{1,0:T(8,128)(2,1)} %bitcast.7, bf16[288,1536]{1,0:T(8,128)(2,1)} %bitcast.8, f32[384]{0:T(512)} %refs_2_.1, f32[384]{0:T(512)} %refs_3_.1, f32[288,128]{1,0:T(8,128)} %broadcast_in_dim.8.refs_4_, bf16[96,1152]{1,0:T(8,128)(2,1)} %bitcast.6, ...), custom_call_target="tpu_custom_call" | custom-call | tf_op jit(solution)/shard_map/pallas_call | solution.py:461
  79.1 0.0 copy-start
  79.1 1.9 %copy.14 = bf16[1,2,144,768]{3,2,1,0:T(8,128)(2,1)} copy(bf16[1,2,144,768]{3,2,1,0:T(8,128)(2,1)} %bitcast.10) | data formatting | bytes 884736
  81.0 0.0 copy-done
  81.0 0.8 copy.15
  (1 shorter events, 0.0 us)
Async XLA Ops:
  0.6 0.7 copy-start.1
  79.1 1.9 %copy-start = (bf16[288,768]{1,0:T(8,128)(2,1)S(1)}, bf16[288,768]{1,0:T(8,128)(2,1)}, u32[]{:S(2)}) copy-start(bf16[288,768]{1,0:T(8,128)(2,1)} %get-tuple-element.5) | copy-start | bytes 1327108
